TPU v7x, 32 devices: a whole 2x2x4 slice. The times are simulated.
32 devices in a mesh: dp: 8 (over z, x), tensor: 4 (over y, core).
Axes of the slice: x: 2, y: 2, z: 4, core: 2. Of those that a mesh axis runs over, the one named last changes fastest.
Arguments:
- tokens: bfloat16 [8, 1024, 768], P('dp', 'tensor'), may hold values from -6 to 6
- segment_ids: int32 [8, 1024], P('dp'), may hold values from 0 to 2, as said below
- mix_norm_gain: float32 [768], replicated, may hold values from 0.5 to 1.5
- mix_norm_bias: float32 [768], replicated, may hold values from -3 to 3
- in_weight: bfloat16 [768, 3, 768], P('dp', None, 'tensor'), may hold values from -0.21875 to 0.21875
- in_bias: float32 [3, 768], P(None, 'tensor'), may hold values from -3 to 3
- short_weight: float32 [3, 3, 768], P(None, None, 'tensor'), may hold values from -3.5 to 3.5
- short_bias: float32 [3, 768], P(None, 'tensor'), may hold values from -3 to 3
- filt_in_weight: float32 [33, 64], replicated, may hold values from -1 to 1
- filt_in_bias: float32 [64], replicated, may hold values from -4 to 4
- filt_mid_weight: float32 [64, 64], replicated, may hold values from -0.75 to 0.75
- filt_mid_bias: float32 [64], replicated, may hold values from -4 to 4
- filt_out_weight: float32 [64, 2, 768], P(None, None, 'tensor'), may hold values from -0.125 to 0.125
- decay_rates: float32 [2, 768], P(None, 'tensor'), may hold values from 0.0005 to 0.15
- long_bias: float32 [2, 768], P(None, 'tensor'), may hold values from -4 to 4
- out_weight: bfloat16 [768, 768], P('dp', 'tensor'), may hold values from -0.21875 to 0.21875
- out_bias: float32 [768], replicated, may hold values from -3 to 3
- mlp_norm_gain: float32 [768], replicated, may hold values from 0.5 to 1.5
- mlp_norm_bias: float32 [768], replicated, may hold values from -3 to 3
- up_weight: bfloat16 [768, 3072], P('dp', 'tensor'), may hold values from -0.21875 to 0.21875
- up_bias: float32 [3072], P('tensor'), may hold values from -3 to 3
- down_weight: bfloat16 [768, 3072], P('dp', 'tensor'), may hold values from -0.109375 to 0.109375
- down_bias: float32 [768], replicated, may hold values from -3 to 3
- cotangent: bfloat16 [8, 1024, 768], P('dp', 'tensor'), may hold values from -6 to 6
Outputs:
- output: bfloat16 [8, 1024, 768], P('dp', 'tensor')
- grad_tokens: bfloat16 [8, 1024, 768], P('dp', 'tensor')
- grad_mix_norm_gain: float32 [768], replicated
- grad_mix_norm_bias: float32 [768], replicated
- grad_in_weight: float32 [768, 3, 768], P('dp', None, 'tensor')
- grad_in_bias: float32 [3, 768], P(None, 'tensor')
- grad_short_weight: float32 [3, 3, 768], P(None, None, 'tensor')
- grad_short_bias: float32 [3, 768], P(None, 'tensor')
- grad_filt_in_weight: float32 [33, 64], replicated
- grad_filt_in_bias: float32 [64], replicated
- grad_filt_mid_weight: float32 [64, 64], replicated
- grad_filt_mid_bias: float32 [64], replicated
- grad_filt_out_weight: float32 [64, 2, 768], P(None, None, 'tensor')
- grad_long_bias: float32 [2, 768], P(None, 'tensor')
- grad_out_weight: float32 [768, 768], P('dp', 'tensor')
- grad_out_bias: float32 [768], replicated
- grad_mlp_norm_gain: float32 [768], replicated
- grad_mlp_norm_bias: float32 [768], replicated
- grad_up_weight: float32 [768, 3072], P('dp', 'tensor')
- grad_up_bias: float32 [3072], P('tensor')
- grad_down_weight: float32 [768, 3072], P('dp', 'tensor')
- grad_down_bias: float32 [768], replicated
Inputs may be any that keep to these rules, and one draw needn't show every extreme that they name: `segment_ids`: ids never fall along a sequence and every sequence holds all 3 documents: document 0 covers the first 1 to 64 positions, document 2 the last 1 to 64, document 1 all positions between.
All inputs are finite; a program needn't handle non-finite values.
Results may differ from a plain program's by a relative error of at most 0.0055.
The roundings to bfloat16 on the way count: a program that leaves them out, or rounds other values in their place, can miss the bound.
Values may be sent and summed in bfloat16 or wider, within the bound.
A program may use at most 256 MiB of HBM per device.

v0:
```python
import math

import jax
import jax.numpy as jnp
from jax import lax
from jax.sharding import PartitionSpec as P

DOCS = 3
FFT_A = 32


EPSILON = 1e-05
HIGHEST = lax.Precision.HIGHEST
ROW_CONTRACT = (((1,), (1,)), ((), ()))
COLUMN_CONTRACT = (((0,), (0,)), ((), ()))


def layer_norm(values, norm_gain, norm_shift):
    center = jnp.mean(values, axis=-1, keepdims=True)
    centred = values - center
    spread = jnp.mean(centred * centred, axis=-1, keepdims=True)
    return centred * lax.rsqrt(spread + EPSILON) * norm_gain + norm_shift


def smooth_gelu(values):
    return jax.nn.gelu(values, approximate=True)


def position_table(length, emb_width):
    band_count = (emb_width - 1) // 2
    places = jnp.arange(length, dtype=jnp.float32)
    angles = 2.0 * math.pi * places / length
    frequency = jnp.linspace(0.0001, band_count - 1, band_count, dtype=jnp.float32)
    phases = angles[:, None] * frequency[None, :]
    return jnp.concatenate(
        [(places / (length - 1))[:, None], jnp.cos(phases), -jnp.sin(phases)], axis=1
    )


def make_filter(table, first_weight, first_bias, middle_weight, middle_bias, last_weight, rates):
    hidden = jnp.sin(jnp.dot(table, first_weight, precision=HIGHEST) + first_bias)
    hidden = jnp.sin(jnp.dot(hidden, middle_weight, precision=HIGHEST) + middle_bias)
    raw_filter = jnp.einsum("tk,koc->toc", hidden, last_weight, precision=HIGHEST)
    places = jnp.arange(table.shape[0], dtype=jnp.float32)
    return raw_filter * jnp.exp(-places[:, None, None] * rates[None])


def short_conv(values, doc_ids, taps, tap_bias):
    running = tap_bias[None] + taps[0][None] * values
    for offset in range(1, taps.shape[0]):
        shifted = jnp.concatenate([jnp.zeros_like(values[:offset]), values[:-offset]], axis=0)
        same_doc = jnp.concatenate(
            [
                jnp.zeros((offset,), jnp.float32),
                (doc_ids[offset:] == doc_ids[:-offset]).astype(jnp.float32),
            ]
        )
        running = running + taps[offset][None] * shifted * same_doc[:, None, None]
    return running


def dft_tables(size_a, size_b):
    size_all = size_a * size_b
    index_a = jnp.arange(size_a, dtype=jnp.int32)
    index_b = jnp.arange(size_b, dtype=jnp.int32)
    turn = 2.0 * math.pi
    angle_a = turn * (index_a[:, None] * index_a[None, :] % size_a).astype(jnp.float32) / size_a
    angle_b = turn * (index_b[:, None] * index_b[None, :] % size_b).astype(jnp.float32) / size_b
    angle_tw = (
        turn * (index_a[:, None] * index_b[None, :] % size_all).astype(jnp.float32) / size_all
    )
    fa_real = jnp.cos(angle_a)
    fa_imag = -jnp.sin(angle_a)
    fb_real = jnp.cos(angle_b)
    fb_imag = -jnp.sin(angle_b)
    first_table = jnp.concatenate([fa_real, fa_imag], axis=0)
    block_table = jnp.concatenate(
        [jnp.concatenate([fb_real, -fb_imag], axis=1), jnp.concatenate([fb_imag, fb_real], axis=1)],
        axis=0,
    )
    last_table = jnp.concatenate([fa_real, fa_imag], axis=1)
    return (first_table, block_table, last_table, jnp.cos(angle_tw), -jnp.sin(angle_tw))


def forward_dft(signal, dft_tabs):
    first_table, block_table, last_table, tw_real, tw_imag = dft_tabs
    size_a = tw_real.shape[0]
    half_a = signal.shape[0]
    section = jnp.einsum("kn,nqw->kqw", first_table[:, :half_a], signal, precision=HIGHEST)
    section_real = section[:size_a]
    section_imag = section[size_a:]
    turned_real = section_real * tw_real[:, :, None] - section_imag * tw_imag[:, :, None]
    turned_imag = section_real * tw_imag[:, :, None] + section_imag * tw_real[:, :, None]
    turned = jnp.concatenate([turned_real, turned_imag], axis=1)
    return jnp.einsum("pq,kqw->kpw", block_table, turned, precision=HIGHEST)


def inverse_dft(spectrum, dft_tabs):
    first_table, block_table, last_table, tw_real, tw_imag = dft_tabs
    size_a, size_b = tw_real.shape
    half_a = size_a // 2
    inner = jnp.einsum("qp,kqw->kpw", block_table, spectrum, precision=HIGHEST)
    inner_real = inner[:, :size_b]
    inner_imag = inner[:, size_b:]
    turned_real = inner_real * tw_real[:, :, None] + inner_imag * tw_imag[:, :, None]
    turned_imag = inner_imag * tw_real[:, :, None] - inner_real * tw_imag[:, :, None]
    turned = jnp.concatenate([turned_real, turned_imag], axis=0)
    outcome = jnp.einsum("nk,kqw->nqw", last_table[:half_a], turned, precision=HIGHEST)
    return outcome / (size_a * size_b)


def long_conv(signal, filt_one, direct, doc_masks, dft_tabs):
    length, width = signal.shape
    doc_count = doc_masks.shape[1]
    size_a, size_b = dft_tabs[3].shape
    half_a = size_a // 2
    pieces = (doc_masks[:, :, None] * signal[:, None, :]).reshape(half_a, size_b, doc_count * width)
    filt_spec = forward_dft(filt_one.reshape(half_a, size_b, width), dft_tabs)
    spectrum = forward_dft(pieces, dft_tabs).reshape(size_a, 2 * size_b, doc_count, width)
    spec_real = spectrum[:, :size_b]
    spec_imag = spectrum[:, size_b:]
    filt_real = filt_spec[:, :size_b, None, :]
    filt_imag = filt_spec[:, size_b:, None, :]
    product = jnp.concatenate(
        [
            spec_real * filt_real - spec_imag * filt_imag,
            spec_real * filt_imag + spec_imag * filt_real,
        ],
        axis=1,
    )
    result = inverse_dft(product.reshape(size_a, 2 * size_b, doc_count * width), dft_tabs).reshape(
        length, doc_count, width
    )
    return jnp.sum(doc_masks[:, :, None] * result, axis=1) + direct * signal


def body(
    tokens,
    segment_ids,
    mix_norm_gain,
    mix_norm_bias,
    in_weight,
    in_bias,
    short_weight,
    short_bias,
    filt_in_weight,
    filt_in_bias,
    filt_mid_weight,
    filt_mid_bias,
    filt_out_weight,
    decay_rates,
    long_bias,
    out_weight,
    out_bias,
    mlp_norm_gain,
    mlp_norm_bias,
    up_weight,
    up_bias,
    down_weight,
    down_bias,
    cotangent,
):
    residual = tokens[0].astype(jnp.float32)
    doc_ids = segment_ids[0]
    model_width = residual.shape[1]
    length = doc_ids.shape[0]
    in_all, out_all, up_all, down_all = (
        lax.all_gather(in_weight, "dp", axis=0, tiled=True),
        lax.all_gather(out_weight, "dp", axis=0, tiled=True),
        lax.all_gather(up_weight, "dp", axis=0, tiled=True),
        lax.all_gather(down_weight, "dp", axis=0, tiled=True),
    )
    channels = in_all.shape[2]
    in_flat = in_all.reshape(model_width, 3 * channels)

    def take_rows(weight_flat, incoming):
        product = jnp.dot(incoming, weight_flat, preferred_element_type=jnp.float32)
        return (product, incoming)

    def back_rows(weight_all, kept_low, incoming):
        product = jnp.dot(incoming, weight_all, preferred_element_type=jnp.float32)
        weight_grad = lax.dot_general(
            incoming, kept_low, COLUMN_CONTRACT, preferred_element_type=jnp.float32
        )
        return (product, weight_grad)

    def sum_terms(left_low, weight_all):
        return lax.dot_general(
            left_low, weight_all, ROW_CONTRACT, preferred_element_type=jnp.float32
        )

    normed, first_norm_back = jax.vjp(layer_norm, residual, mix_norm_gain, mix_norm_bias)
    normed_low = normed.astype(jnp.bfloat16)
    projected, normed_full = take_rows(
        in_flat, lax.all_gather(normed_low, "tensor", axis=0, tiled=True)
    )
    zvalue = projected.reshape(length, 3, channels) + in_bias
    table = position_table(length, filt_in_weight.shape[0])
    doc_masks = (doc_ids[:, None] == jnp.arange(DOCS, dtype=jnp.int32)[None, :]).astype(jnp.float32)
    dft_tabs = dft_tables(FFT_A, 2 * length // FFT_A)

    def mixer_core(
        conv_input,
        taps,
        tap_bias,
        first_weight,
        first_bias,
        middle_weight,
        middle_bias,
        last_weight,
        direct,
    ):
        local_conv = short_conv(conv_input, doc_ids, taps, tap_bias)
        filters = make_filter(
            table, first_weight, first_bias, middle_weight, middle_bias, last_weight, decay_rates
        )
        first = local_conv[:, 1] * long_conv(
            local_conv[:, 0], filters[:, 0], direct[0], doc_masks, dft_tabs
        )
        return local_conv[:, 2] * long_conv(first, filters[:, 1], direct[1], doc_masks, dft_tabs)

    gated_out, mixer_back = jax.vjp(
        mixer_core,
        zvalue,
        short_weight,
        short_bias,
        filt_in_weight,
        filt_in_bias,
        filt_mid_weight,
        filt_mid_bias,
        filt_out_weight,
        long_bias,
    )
    gated_low = gated_out.astype(jnp.bfloat16)
    own_gated = lax.all_to_all(gated_low, "tensor", split_axis=0, concat_axis=1, tiled=True)
    out_full = lax.all_gather(out_all, "tensor", axis=1, tiled=True)
    mixed = lax.dot_general(own_gated, out_full, ROW_CONTRACT, preferred_element_type=jnp.float32)
    mixed_sum = residual + mixed + out_bias
    normed_two, second_norm_back = jax.vjp(layer_norm, mixed_sum, mlp_norm_gain, mlp_norm_bias)
    normed_two_low = normed_two.astype(jnp.bfloat16)
    up_raw, normed_two_full = take_rows(
        up_all, lax.all_gather(normed_two_low, "tensor", axis=0, tiled=True)
    )
    pre_act = up_raw + up_bias
    activated, gelu_back = jax.vjp(smooth_gelu, pre_act)
    act_low = activated.astype(jnp.bfloat16)
    mlp_sum = lax.psum_scatter(
        sum_terms(act_low, down_all), "tensor", scatter_dimension=0, tiled=True
    )
    output = (mixed_sum + mlp_sum + down_bias).astype(jnp.bfloat16)
    grad_low = cotangent[0]
    grad_out = grad_low.astype(jnp.float32)
    grad_down_bias = jnp.sum(grad_out, axis=0)
    d_act, grad_down = back_rows(
        down_all, act_low, lax.all_gather(grad_low, "tensor", axis=0, tiled=True)
    )
    d_pre_low = gelu_back(d_act)[0].astype(jnp.bfloat16)
    grad_up_bias = jnp.sum(d_pre_low, axis=0, dtype=jnp.float32)
    grad_up = lax.dot_general(
        normed_two_full, d_pre_low, COLUMN_CONTRACT, preferred_element_type=jnp.float32
    )
    d_normed_two = lax.psum_scatter(
        sum_terms(d_pre_low, up_all), "tensor", scatter_dimension=0, tiled=True
    )
    d_mixed_norm, grad_mlp_gain, grad_mlp_shift = second_norm_back(d_normed_two)
    d_mixed = grad_out + d_mixed_norm
    grad_out_bias = jnp.sum(d_mixed, axis=0)
    d_mix_low = d_mixed.astype(jnp.bfloat16)
    d_gated, grad_out_w = back_rows(
        out_all, gated_low, lax.all_gather(d_mix_low, "tensor", axis=0, tiled=True)
    )
    (
        d_zvalue,
        grad_taps,
        grad_tap_bias,
        grad_first_w,
        grad_first_b,
        grad_middle_w,
        grad_middle_b,
        grad_last_w,
        grad_direct,
    ) = mixer_back(d_gated)
    d_z_low = d_zvalue.reshape(length, 3 * channels).astype(jnp.bfloat16)
    grad_in_bias = jnp.sum(d_z_low, axis=0, dtype=jnp.float32).reshape(3, channels)
    grad_in = lax.dot_general(
        normed_full, d_z_low, COLUMN_CONTRACT, preferred_element_type=jnp.float32
    ).reshape(model_width, 3, channels)
    d_normed = lax.psum_scatter(
        sum_terms(d_z_low, in_flat), "tensor", scatter_dimension=0, tiled=True
    )
    d_input_norm, grad_mix_gain, grad_mix_shift = first_norm_back(d_normed)
    grad_tokens = (d_mixed + d_input_norm).astype(jnp.bfloat16)[None]
    grad_in, grad_out_w, grad_up, grad_down = (
        lax.psum_scatter(grad_in, "dp", scatter_dimension=0, tiled=True),
        lax.psum_scatter(grad_out_w, "dp", scatter_dimension=0, tiled=True),
        lax.psum_scatter(grad_up, "dp", scatter_dimension=0, tiled=True),
        lax.psum_scatter(grad_down, "dp", scatter_dimension=0, tiled=True),
    )
    grad_in_bias, grad_taps, grad_tap_bias, grad_last_w, grad_direct, grad_up_bias = lax.psum(
        (grad_in_bias, grad_taps, grad_tap_bias, grad_last_w, grad_direct, grad_up_bias), "dp"
    )
    (
        grad_mix_gain,
        grad_mix_shift,
        grad_first_w,
        grad_first_b,
        grad_middle_w,
        grad_middle_b,
        grad_out_bias,
        grad_mlp_gain,
        grad_mlp_shift,
        grad_down_bias,
    ) = lax.psum(
        (
            grad_mix_gain,
            grad_mix_shift,
            grad_first_w,
            grad_first_b,
            grad_middle_w,
            grad_middle_b,
            grad_out_bias,
            grad_mlp_gain,
            grad_mlp_shift,
            grad_down_bias,
        ),
        ("dp", "tensor"),
    )
    return (
        output[None],
        grad_tokens,
        grad_mix_gain,
        grad_mix_shift,
        grad_in,
        grad_in_bias,
        grad_taps,
        grad_tap_bias,
        grad_first_w,
        grad_first_b,
        grad_middle_w,
        grad_middle_b,
        grad_last_w,
        grad_direct,
        grad_out_w,
        grad_out_bias,
        grad_mlp_gain,
        grad_mlp_shift,
        grad_up,
        grad_up_bias,
        grad_down,
        grad_down_bias,
    )


def solution(mesh):
    placed = (
        P("dp", "tensor", None),
        P("dp", None),
        P(),
        P(),
        P("dp", None, "tensor"),
        P(None, "tensor"),
        P(None, None, "tensor"),
        P(None, "tensor"),
        P(),
        P(),
        P(),
        P(),
        P(None, None, "tensor"),
        P(None, "tensor"),
        P(None, "tensor"),
        P("dp", "tensor"),
        P(),
        P(),
        P(),
        P("dp", "tensor"),
        P("tensor"),
        P("dp", "tensor"),
        P(),
        P("dp", "tensor", None),
    )
    return jax.shard_map(
        body,
        mesh=mesh,
        in_specs=placed,
        out_specs=(
            P("dp", "tensor", None),
            P("dp", "tensor", None),
            P(),
            P(),
            P("dp", None, "tensor"),
            P(None, "tensor"),
            P(None, None, "tensor"),
            P(None, "tensor"),
            P(),
            P(),
            P(),
            P(),
            P(None, None, "tensor"),
            P(None, "tensor"),
            P("dp", "tensor"),
            P(),
            P(),
            P(),
            P("dp", "tensor"),
            P("tensor"),
            P("dp", "tensor"),
            P(),
        ),
        check_vma=False,
    )
```

profile of v0, /device:TPU:1, one launch (start us, length us, event | category | flops | bytes accessed | tf_op | source)
XLA Modules:
  0.0 1346.1 jit_solution(5550607090076465014)
XLA Ops:
  11.9 26.4 %all_gather.29 = bf16[768,192]{1,0:T(8,128)(2,1)S(1)} all-gather(bf16[96,192]{1,0:T(8,128)(2,1)} %param.39), channel_id=1, replica_groups=mesh['dp'=8,'tensor'=4] {'dp'}, dimensions={0}, use_global_device_ids=true | all-gather | bytes 331776 | tf_op jit(solution)/shard_map/all_gather | solution.py:169
  42.2 30.1 %all_gather.28 = bf16[768,3,192]{2,0,1:T(8,128)(2,1)S(1)} all-gather(bf16[96,3,192]{2,0,1:T(8,128)(2,1)S(1)} %copy-done.42), channel_id=1, replica_groups=mesh['dp'=8,'tensor'=4] {'dp'}, dimensions={0}, use_global_device_ids=true | all-gather | bytes 995328 | tf_op jit(solution)/shard_map/all_gather | solution.py:168
  168.8 20.7 %fusion.14 = f32[32,576,128]{2,1,0:T(8,128)S(1)} fusion(f32[128,128,1]{1,0,2:T(8,128)S(1)} %maximum_bitcast_fusion, f32[32,128,576]{2,0,1:T(8,128)} %pad_maximum_fusion), kind=kOutput, calls=%fused_computation.16 | convolution fusion | flops 3623878656 | bytes 18939904 | tf_op jit(solution)/shard_map/jvp(pq,kqw->kpw)/dot_general | solution.py:95
  198.8 12.5 pad_maximum_fusion.2
  211.3 11.8 fusion.191
  223.1 12.1 copy.183
  305.6 20.7 %fusion.12 = f32[32,576,128]{2,1,0:T(8,128)S(1)} fusion(f32[128,128,1]{1,0,2:T(8,128)S(1)} %maximum_bitcast_fusion, f32[32,128,576]{2,0,1:T(8,128)} %pad_maximum_fusion.1), kind=kOutput, calls=%fused_computation.14 | convolution fusion | flops 3623878656 | bytes 18939904 | tf_op jit(solution)/shard_map/jvp(pq,kqw->kpw)/dot_general | solution.py:95
  335.7 12.5 pad_maximum_fusion.3
  348.2 11.8 fusion.192
  360.0 12.2 copy.193
  404.6 15.0 %all-to-all-start = ((bf16[4,256,192]{1,2,0:T(8,128)(2,1)}), bf16[4,256,192]{1,2,0:T(8,128)(2,1)}, u32[]{:S(2)}, u32[]{:S(2)}) async-start(bf16[4,256,192]{1,2,0:T(8,128)(2,1)} %fusion.107), calls=%async_computation | async-start | bytes 786432 | tf_op jit(solution)/shard_map/all_to_all | solution.py:235
  431.4 19.4 %all-gather.13.cloned.1.call-done = bf16[1024,768]{1,0:T(8,128)(2,1)} async-done(((bf16[256,768]{1,0:T(8,128)(2,1)}), bf16[1024,768]{1,0:T(8,128)(2,1)}) %all-gather.13.cloned.1.call-update) | async-done | bytes 1572880 | tf_op jit(solution)/shard_map/all_gather | solution.py:242
  455.6 36.6 %all-gather.17.cloned.1.call-done = bf16[768,768]{1,0:T(8,128)(2,1)} async-done(((bf16[96,768]{1,0:T(8,128)(2,1)}), bf16[768,768]{1,0:T(8,128)(2,1)}) %all-gather.17.cloned.1.call-update) | async-done | bytes 1179664 | tf_op jit(solution)/shard_map/all_gather | solution.py:171
  492.2 21.5 %all-gather.21.cloned.1.call-done = bf16[1,1024,768]{2,1,0:T(8,128)(2,1)} async-done(((bf16[1,256,768]{2,1,0:T(8,128)(2,1)}), bf16[1,1024,768]{2,1,0:T(8,128)(2,1)}) %all-gather.21.cloned.1.call-update) | async-done | bytes 1572880 | tf_op jit(solution)/shard_map/all_gather | solution.py:255
  530.5 31.6 %reduce-scatter.12.cloned.1.call-done = f32[256,768]{1,0:T(8,128)} async-done(((f32[1024,768]{1,0:T(8,128)}), f32[256,768]{1,0:T(8,128)}) %reduce-scatter.12.cloned.1.call-update) | async-done | bytes 786448 | tf_op jit(solution)/shard_map/reduce_scatter | solution.py:262
  565.7 37.1 %reduce-scatter.10.cloned.1.call-done = f32[256,768]{1,0:T(8,128)} async-done(((f32[1024,768]{1,0:T(8,128)}), f32[256,768]{1,0:T(8,128)}) %reduce-scatter.10.cloned.1.call-update) | async-done | bytes 786448 | tf_op jit(solution)/shard_map/reduce_scatter | solution.py:247
  610.5 17.7 %all-gather.19.cloned.1.call-done = bf16[1024,768]{1,0:T(8,128)(2,1)} async-done(((bf16[256,768]{1,0:T(8,128)(2,1)}), bf16[1024,768]{1,0:T(8,128)(2,1)}) %all-gather.19.cloned.1.call-update) | async-done | bytes 1572880 | tf_op jit(solution)/shard_map/all_gather | solution.py:270
  670.7 21.6 %fusion.10 = f32[32,576,128]{2,1,0:T(8,128)} fusion(f32[128,128,1]{1,0,2:T(8,128)S(1)} %maximum_bitcast_fusion, f32[32,576,128]{1,0,2:T(8,128)} %add_bitcast_fusion.1), kind=kOutput, calls=%fused_computation.12 | convolution fusion | flops 3623878656 | bytes 18939904 | tf_op jit(solution)/shard_map/transpose(jvp(qp,kqw->kpw))/dot_general | solution.py:102
  692.3 31.9 %multiply_reduce_fusion.6 = (f32[32,64,192]{1,2,0:T(8,128)}, f32[32,64,192]{1,2,0:T(8,128)}, f32[32,64,192]{1,2,0:T(8,128)}, f32[32,64,192]{1,2,0:T(8,128)}, f32...) fusion(f32[32,128,3,192]{1,3,2,0:T(8,128)} %bitcast.260, f32[32,128,3,192]{1,3,2,0:T(8,128)} %bitcast.259, ...), kind=kLoop, calls=%fused_computation.36 | loop fusion | flops 16121856 | bytes 37748736 | tf_op jit(solution)/shard_map/transpose(jvp())/reduce_sum | solution.py:126
  739.0 12.5 pad_add_fusion.1
  751.5 11.8 fusion.195
  763.4 12.1 copy.208
  847.5 21.7 %fusion.8 = f32[32,576,128]{2,1,0:T(8,128)} fusion(f32[128,128,1]{1,0,2:T(8,128)S(1)} %maximum_bitcast_fusion, f32[32,576,128]{1,0,2:T(8,128)} %add_bitcast_fusion), kind=kOutput, calls=%fused_computation.10 | convolution fusion | flops 3623878656 | bytes 18939904 | tf_op jit(solution)/shard_map/transpose(jvp(qp,kqw->kpw))/dot_general | solution.py:102
  869.2 32.3 %multiply_reduce_fusion.2 = (f32[32,64,192]{1,2,0:T(8,128)}, f32[32,64,192]{1,2,0:T(8,128)}, f32[32,64,192]{1,2,0:T(8,128)}, f32[32,64,192]{1,2,0:T(8,128)}, f32...) fusion(f32[32,128,3,192]{1,3,2,0:T(8,128)} %bitcast.261, f32[32,128,3,192]{1,3,2,0:T(8,128)} %bitcast.257, ...), kind=kLoop, calls=%fused_computation.32 | loop fusion | flops 16121856 | bytes 37748736 | tf_op jit(solution)/shard_map/transpose(jvp())/reduce_sum | solution.py:126
  940.1 12.5 pad_add_fusion
  952.7 11.7 fusion.196
  964.4 12.2 copy.215
  1042.3 31.0 %all-reduce.36 = (f32[3,192]{1,0:T(4,128)}, f32[3,3,192]{2,1,0:T(4,128)}, f32[3,192]{1,0:T(4,128)}, f32[2,192]{1,0:T(2,128)}, f32[768]{0:T(1024)}) all-reduce(f32[3,192]{1,0:T(4,128)S(1)} %get-tuple-element.196, f32[3,3,192]{2,1,0:T(4,128)S(1)} %pad_add_fusion.3, ...), channel_id=1, replica_groups=mesh['dp'=8,'tensor'=4] {'dp'}, use_global_device_ids=true, to_apply=%region_21.22 | all-reduce | flops 4032 | bytes 32256 | tf_op jit(solution)/shard_map/psum | solution.py:299
  1083.8 46.5 %all-reduce.35 = (f32[768]{0:T(1024)}, f32[768]{0:T(1024)}, f32[33,64]{1,0:T(8,128)}, f32[64]{0:T(128)}, f32[64,64]{1,0:T(8,128)}, /*index=5*/f32[64]{0:T(128)},...) all-reduce(f32[768]{0:T(1024)S(1)} %get-tuple-element.124, ...), channel_id=1, replica_groups=mesh['dp'=8,'tensor'=4] {'dp','tensor'}, use_global_device_ids=true, to_apply=%region_16.17 | all-reduce | flops 10944 | bytes 87552 | tf_op jit(solution)/shard_map/psum | solution.py:313
  1132.5 69.0 %reduce-scatter.22.cloned.1.call-done = f32[96,768]{1,0:T(8,128)} async-done(((f32[768,768]{1,0:T(8,128)}), f32[96,768]{1,0:T(8,128)}) %reduce-scatter.22.cloned.1.call-update) | async-done | bytes 294928
  1201.6 64.6 %reduce-scatter.18.cloned.1.call-done = f32[96,192]{1,0:T(8,128)} async-done(((f32[768,192]{1,0:T(8,128)}), f32[96,192]{1,0:T(8,128)}) %reduce-scatter.18.cloned.1.call-update) | async-done | bytes 73744 | tf_op jit(solution)/shard_map/reduce_scatter | solution.py:295
  1266.1 73.0 %reduce-scatter.16.cloned.1.call-done = f32[96,3,192]{2,0,1:T(8,128)} async-done(((f32[768,3,192]{2,0,1:T(8,128)}), f32[96,3,192]{2,0,1:T(8,128)}) %reduce-scatter.16.cloned.1.call-update) | async-done | bytes 221200 | tf_op jit(solution)/shard_map/reduce_scatter | solution.py:294
  (386 shorter events, 516.2 us)
Async XLA Ops:
  7.2 71.7 %copy-start = (f32[64,2,192]{2,1,0:T(2,128)S(1)}, f32[64,2,192]{2,1,0:T(2,128)}, u32[]{:S(2)}) copy-start(f32[64,2,192]{2,1,0:T(2,128)} %param.36) | copy-start | bytes 294916
  7.2 111.5 %all-gather.9.cloned.1.call-start = ((), (), s32[]{:S(2)}) async-start(), calls=%async_computation.8 | async-start | bytes 1966080 | tf_op jit(solution)/shard_map/all_gather | solution.py:195
  8.5 65.4 %copy-start.47 = (f32[256]{0:T(256)}, f32[256]{0:T(256)S(1)}, u32[]{:S(2)}) copy-start(f32[256]{0:T(256)S(1)} %broadcast_multiply_fusion.5) | copy-start | bytes 3076
  11.8 62.5 %copy-start.65 = (f32[33,64]{1,0:T(8,128)S(1)}, f32[33,64]{1,0:T(8,128)}, u32[]{:S(2)}) copy-start(f32[33,64]{1,0:T(8,128)} %param.32) | copy-start | bytes 25348
  11.8 62.5 %copy-start.89 = (f32[64]{0:T(128)S(1)}, f32[64]{0:T(128)}, u32[]{:S(2)}) copy-start(f32[64]{0:T(128)} %param.33) | copy-start | bytes 772
  11.8 407.7 %all-gather.11.cloned.1.call-start = ((), (), s32[]{:S(2)}) async-start(), calls=%async_computation.9 | async-start | bytes 1474560 | tf_op jit(solution)/shard_map/all_gather | solution.py:236
  39.2 39.7 %copy-start.86 = (f32[2,192]{1,0:T(2,128)S(1)}, f32[2,192]{1,0:T(2,128)}, u32[]{:S(2)}) copy-start(f32[2,192]{1,0:T(2,128)} %param.37) | copy-start | bytes 4612
  39.2 392.2 %all-gather.15.cloned.1.call-start = ((), (), s32[]{:S(2)}) async-start(), calls=%async_computation.11 | async-start | bytes 1327104 | tf_op jit(solution)/shard_map/all_gather | solution.py:170
  40.2 40.2 %copy-start.71 = (f32[1024]{0:T(1024)}, f32[1024]{0:T(1024)S(1)}, u32[]{:S(2)}) copy-start(f32[1024]{0:T(1024)S(1)} %iota_negate_fusion) | copy-start | bytes 12292
  40.2 40.2 %copy-start.49 = (f32[1024,1]{0,1:T(1,128)}, f32[1024,1]{0,1:T(1,128)S(1)}, u32[]{:S(2)}) copy-start(f32[1024,1]{0,1:T(1,128)S(1)} %iota_multiply_fusion.1) | copy-start | bytes 12292
  40.5 336.6 %copy-start.35 = (f32[32,32]{0,1:T(8,128)}, f32[32,32]{0,1:T(8,128)S(1)}, u32[]{:S(2)}) copy-start(f32[32,32]{0,1:T(8,128)S(1)} %get-tuple-element.240) | copy-start | bytes 12292
  83.4 198.0 %copy-start.33 = (f32[64,16,1]{0,1,2:T(8,128)}, f32[64,16,1]{0,1,2:T(8,128)S(1)}, u32[]{:S(2)}) copy-start(f32[64,16,1]{0,1,2:T(8,128)S(1)} %fusion.153) | copy-start | bytes 12292
  404.6 21.5 %all-to-all-start = ((bf16[4,256,192]{1,2,0:T(8,128)(2,1)}), bf16[4,256,192]{1,2,0:T(8,128)(2,1)}, u32[]{:S(2)}, u32[]{:S(2)}) async-start(bf16[4,256,192]{1,2,0:T(8,128)(2,1)} %fusion.107), calls=%async_computation | async-start | bytes 786432 | tf_op jit(solution)/shard_map/all_to_all | solution.py:235
  419.6 31.2 %all-gather.13.cloned.1.call-start = ((), (), s32[]{:S(2)}) async-start(), calls=%async_computation.10 | async-start | bytes 1966080 | tf_op jit(solution)/shard_map/all_gather | solution.py:242
  429.9 62.3 %all-gather.17.cloned.1.call-start = ((), (), s32[]{:S(2)}) async-start(), calls=%async_computation.12 | async-start | bytes 1327104 | tf_op jit(solution)/shard_map/all_gather | solution.py:171
  430.5 83.2 %all-gather.21.cloned.1.call-start = ((), (), s32[]{:S(2)}) async-start(), calls=%async_computation.21 | async-start | bytes 1966080 | tf_op jit(solution)/shard_map/all_gather | solution.py:255
  431.1 82.7 %copy-start.93 = (f32[768]{0:T(1024)S(1)}, f32[768]{0:T(1024)}, u32[]{:S(2)}) copy-start(f32[768]{0:T(1024)} %param.44) | copy-start | bytes 9220
  431.1 131.0 %reduce-scatter.12.cloned.1.call-start = ((), (), s32[]{:S(2)}) async-start(), calls=%async_computation.14 | async-start | bytes 3932160 | tf_op jit(solution)/shard_map/reduce_scatter | solution.py:262
  524.4 78.4 %reduce-scatter.10.cloned.1.call-start = ((), (), s32[]{:S(2)}) async-start(), calls=%async_computation.13 | async-start | bytes 3932160 | tf_op jit(solution)/shard_map/reduce_scatter | solution.py:247
  530.5 75.9 %copy-start.19 = (bf16[1,256,768]{2,1,0:T(8,128)(2,1)S(1)}, bf16[1,256,768]{2,1,0:T(8,128)(2,1)}, u32[]{:S(2)}) copy-start(bf16[1,256,768]{2,1,0:T(8,128)(2,1)} %param.47) | copy-start | bytes 1179652
  530.5 97.7 %all-gather.19.cloned.1.call-start = ((), (), s32[]{:S(2)}) async-start(), calls=%async_computation.15 | async-start | bytes 1966080 | tf_op jit(solution)/shard_map/all_gather | solution.py:270
  608.0 471.1 %all-reduce.39.cloned.1.call-start = ((), (), s32[]{:S(2)}) async-start(), calls=%async_computation.18 | async-start | bytes 262144 | tf_op jit(solution)/shard_map/psum | solution.py:299
  939.9 140.8 %reduce-scatter.14.cloned.1.call-start = ((), (), s32[]{:S(2)}) async-start(), calls=%async_computation.16 | async-start | bytes 3932160 | tf_op jit(solution)/shard_map/reduce_scatter | solution.py:288
  1019.6 112.9 %reduce-scatter.20.cloned.1.call-start = ((), (), s32[]{:S(2)}) async-start(), calls=%async_computation.20 | async-start | bytes 2654208 | tf_op jit(solution)/shard_map/reduce_scatter | solution.py:296
  1024.4 177.2 %reduce-scatter.22.cloned.1.call-start = ((), (), s32[]{:S(2)}) async-start(), calls=%async_computation.22 | async-start | bytes 2654208
  1033.8 232.3 %reduce-scatter.18.cloned.1.call-start = ((), (), s32[]{:S(2)}) async-start(), calls=%async_computation.19 | async-start | bytes 884736 | tf_op jit(solution)/shard_map/reduce_scatter | solution.py:295
  1036.9 302.2 %reduce-scatter.16.cloned.1.call-start = ((), (), s32[]{:S(2)}) async-start(), calls=%async_computation.17 | async-start | bytes 2654208 | tf_op jit(solution)/shard_map/reduce_scatter | solution.py:294
  1042.1 38.6 %copy-start.11 = (bf16[1,256,768]{2,1,0:T(8,128)(2,1)S(1)}, bf16[1,256,768]{2,1,0:T(8,128)(2,1)}, u32[]{:S(2)}) copy-start(bf16[1,256,768]{2,1,0:T(8,128)(2,1)} %param.24) | copy-start | bytes 1179652
  1042.2 39.9 %copy-start.79 = (f32[256]{0:T(256)S(1)}, f32[256]{0:T(256)}, u32[]{:S(2)}) copy-start(f32[256]{0:T(256)} %copy-done.78) | copy-start | bytes 3076
  1042.2 40.0 %copy-start.67 = (f32[256]{0:T(256)S(1)}, f32[256]{0:T(256)}, u32[]{:S(2)}) copy-start(f32[256]{0:T(256)} %copy-done.66) | copy-start | bytes 3076
  1073.4 56.9 %copy-start.18 = (f32[256,768]{1,0:T(8,128)S(1)}, f32[256,768]{1,0:T(8,128)}, u32[]{:S(2)}) copy-start(f32[256,768]{1,0:T(8,128)} %copy-done.17) | copy-start | bytes 2359300
  1073.4 56.9 %copy-start.77 = (f32[256]{0:T(256)S(1)}, f32[256]{0:T(256)}, u32[]{:S(2)}) copy-start(f32[256]{0:T(256)} %copy-done.76) | copy-start | bytes 3076
  (80 other events, 1051.3 us)
Sparse Core Ops, SparseCore 0:
  11.9 22.1 all-gather.8
  39.3 24.8 all-gather.10
  66.4 40.7 all-gather.14
  430.0 20.6 all-gather.12
  452.8 39.3 all-gather.16
  493.6 20.0 all-gather.20
  524.5 37.5 reduce-scatter.11
  564.8 37.9 reduce-scatter.9
  608.1 20.0 all-gather.18
  940.0 67.5 all-reduce.38
  1019.7 37.5 reduce-scatter.13
  1061.3 68.0 reduce-scatter.19
  1133.4 68.0 reduce-scatter.21
  1205.3 60.7 reduce-scatter.17
  1270.4 68.6 reduce-scatter.15
where the time goes:
time: 1350 us
  waiting for transfers between devices  379 us (28%)
  other arithmetic  316 us (23%)
  matrix products  300 us (22%)
  local copies, waits for them, and re-layouts  185 us (14%)
  blocking collectives  134 us (10%)
  starting transfers between devices  16.2 us (1%)
  between operations  15.7 us (1%)
    dot_general x8, matrix products, forward_dft(): return jnp.einsum('pq,kqw->kpw', block_table, turned, precision=HIGHEST)  90.9 us
    reduce_scatter x1, waiting for transfers between devices, body(): lax.psum_scatter(grad_in, 'dp', scatter_dimension=0, tiled=True)  73 us
    unnamed x16, waiting for transfers between devices  71 us
    dot_general x4, matrix products, inverse_dft(): inner = jnp.einsum('qp,kqw->kpw', block_table, spectrum, precision=HIGHEST)  66.9 us
    reduce_scatter x1, waiting for transfers between devices, body(): lax.psum_scatter(grad_out_w, 'dp', scatter_dimension=0, tiled=True)  64.6 us
    reduce_sum x2, other arithmetic, long_conv(): spec_imag * filt_imag  64.2 us
    psum x1, blocking collectives, body(): lax.psum((grad_mix_gain, grad_mix_shift, grad_first_w, grad_first_b, grad...  46.5 us
    dot_general x8, matrix products, forward_dft(): jnp.einsum('kn,nqw->kqw', first_table[:, :half_a], signal, precision=HIGH...  45.2 us
  transfers between devices with their start and end apart: 16, of which 10 were waited for; matrix products, arithmetic and copies ran while one was open for 35% of the time, Pallas kernels for 0%

commit v1 on v0

v1 whole, which is shorter than its diff:
```python
import functools
import math

import jax
import jax.numpy as jnp
import numpy as np
from jax import lax
from jax.experimental import pallas as pl
from jax.experimental.pallas import tpu as pltpu
from jax.sharding import PartitionSpec as P

DOCS = 3
EPSILON = 1e-05
HIGHEST = lax.Precision.HIGHEST
ROW_CONTRACT = (((1,), (1,)), ((), ()))
COLUMN_CONTRACT = (((0,), (0,)), ((), ()))
F32, BF16 = jnp.float32, jnp.bfloat16
CHUNK = 64
VMEM_LIMIT = 58 * 2**20


def half_table(count, period):
    turns = ((2 * np.arange(count)[:, None] + 1) * np.arange(count)[None, :]) % (2 * period)
    angle = turns * (math.pi / period)
    return np.cos(angle), -np.sin(angle)


def three_pass(table):
    high = table.astype(np.float32).astype(jnp.bfloat16)
    low = (table.astype(np.float32) - high.astype(np.float32)).astype(jnp.bfloat16)
    return np.concatenate([high, high, low], axis=1)


def wave_tables(length):
    half, edge = length // 2, length // 32
    real, imag = half_table(half, length)
    whole = np.concatenate([real, imag], axis=0)
    e_real, e_imag = half_table(edge, 2 * edge)
    zero = np.zeros_like(e_real)
    both = np.block([[e_real, zero], [zero, e_real], [e_imag, zero], [zero, e_imag]])
    step = (2 * np.arange(half) + 1) * (math.pi / length)
    e_step = np.tile((2 * np.arange(edge) + 1) * (math.pi / (2 * edge)), 2)
    twist = np.stack([np.cos(step), -np.sin(step)], axis=1).astype(np.float32)
    e_twist = np.stack([np.cos(e_step), -np.sin(e_step)], axis=1).astype(np.float32)
    return (
        three_pass(whole), three_pass(whole.T), twist,
        three_pass(both), three_pass(both.T), e_twist,
    )


def position_table(length, emb_width):
    bands = (emb_width - 1) // 2
    places = np.arange(length, dtype=np.float32)
    angles = (2.0 * math.pi * places / length).astype(np.float32)
    frequency = np.linspace(0.0001, bands - 1, bands, dtype=np.float32)
    phases = (angles[:, None] * frequency[None, :]).astype(np.float64)
    table = np.concatenate([(places / (length - 1))[:, None], np.cos(phases), -np.sin(phases)], axis=1)
    return by_parity(table.astype(np.float32))


def by_parity(rows):
    return rows.reshape((rows.shape[0] // 2, 2) + rows.shape[1:]).swapaxes(0, 1)


def in_order(halves):
    return halves.swapaxes(0, 1).reshape((-1,) + halves.shape[2:])


def over_rows(rows, step, work):
    @pl.loop(0, rows // step)
    def _(i):
        work(pl.ds(pl.multiple_of(i * step, step), step))


def parts(x):
    high = x.astype(BF16)
    return high, (x - high.astype(F32)).astype(BF16)


def put_parts(rhs, at, base, block, x):
    high, low = parts(x)
    size = x.shape[0]
    start = at.start if isinstance(at, pl.Slice) else at
    for slot, piece in ((0, high), (1, low), (2, high)):
        rhs[pl.ds(pl.multiple_of(start + (base + slot * block), 16), size), :] = piece


def mul(ar, ai, br, bi):
    return ar * br - ai * bi, ar * bi + ai * br


def mul_conj(ar, ai, br, bi):
    return ar * br + ai * bi, ar * bi - ai * br


def blend(f, x, conj):
    (fe, fo, ft), (xe, xo) = f, x
    m = mul_conj if conj else mul
    if conj:
        a, b = m(*fe, *xe), m(*fo, *xo)
        c, d = m(*fe, *xo), m(*ft, *xe)
    else:
        a, b = m(*fe, *xe), m(*ft, *xo)
        c, d = m(*fe, *xo), m(*fo, *xe)
    return (a[0] + b[0], a[1] + b[1]), (c[0] + d[0], c[1] + d[1])


def dot(a, b):
    return jnp.dot(a, b, preferred_element_type=F32)


def fine_dot(a, b, dims=(((1,), (0,)), ((), ()))):
    return lax.dot_general(a, b, dims, precision=HIGHEST, preferred_element_type=F32)


def analyse(tabs, rhs, source, spec, edge_spec, masks):
    wave, _, _, e_wave, _, _ = tabs
    half, edge = wave.shape[1] // 3, e_wave.shape[1] // 6

    @pl.loop(0, 2)
    def _(par):
        def fill(at):
            put_parts(rhs, at, 0, half, source(par, at) * masks[par, at, 0:1])

        over_rows(half, CHUNK, fill)
        spec[par] = dot(wave[...], rhs[0 : 3 * half, :])
        first, last = pl.ds(0, edge), pl.ds(half - edge, edge)
        window = jnp.concatenate(
            [source(par, first) * masks[par, first, 1:2], source(par, last) * masks[par, last, 2:3]], axis=0
        )
        high, low = parts(window)
        edge_spec[par] = dot(e_wave[...], jnp.concatenate([high, low, high], axis=0))


def pair(ref, index, at, half):
    start = at.start
    return ref[index, at, :], ref[index, pl.ds(pl.multiple_of(start + half, 8), at.size), :]


def spectra_product(tabs, filt, e_filt, spec, e_spec, rhs_even, rhs_odd, conj, turn):
    _, wave_back, twist, _, e_back, e_twist = tabs
    half, edge2 = wave_back.shape[1] // 6, e_back.shape[1] // 6

    def get(f, tw, at, n):
        fe, fo = pair(f, 0, at, n), pair(f, 1, at, n)
        ft = mul(*fo, tw[at, 0:1], tw[at, 1:2]) if turn else pair(f, 2, at, n)
        return fe, fo, ft

    def work(at):
        even, odd = blend(get(filt, twist, at, half), (pair(spec, 0, at, half), pair(spec, 1, at, half)), conj)
        for rhs, (real, imag) in ((rhs_even, even), (rhs_odd, odd)):
            put_parts(rhs, at, 0, 2 * half, real)
            put_parts(rhs, at, half, 2 * half, imag)

    over_rows(half, CHUNK // 2, work)
    at = pl.ds(0, edge2)
    even, odd = blend(get(e_filt, e_twist, at, edge2), (pair(e_spec, 0, at, edge2), pair(e_spec, 1, at, edge2)), conj)
    out = []
    for real, imag in (even, odd):
        high, low = parts(jnp.concatenate([real, imag], axis=0))
        out.append(dot(e_back[...], jnp.concatenate([high, low, high], axis=0)))
    return out


def synthesise(tabs, rhs, out, par):
    out[par, 0 : tabs[1].shape[0], :] = dot(tabs[1][...], rhs[...])


def join(out, edges, direct, source, masks, half):
    for par in range(2):
        def work(at, par=par):
            out[par, at, :] = out[par, at, :] * masks[par, at, 0:1] + direct * source(par, at)

        over_rows(half, CHUNK, work)
        edge = edges[par].shape[0] // 2
        first, last = pl.ds(0, edge), pl.ds(half - edge, edge)
        out[par, first, :] += edges[par][:edge] * masks[par, first, 1:2]
        out[par, last, :] += edges[par][edge:] * masks[par, last, 2:3]


def hidden_layers(table, w1, b1, w2, b2):
    pre1 = fine_dot(table, w1) + b1
    h1 = jnp.sin(pre1)
    pre2 = fine_dot(h1, w2) + b2
    return pre1, h1, pre2


def decay_at(par, rows, start, rates):
    m = lax.broadcasted_iota(jnp.int32, (rows, rates.shape[1]), 0) + start
    return jnp.exp((2 * m + par).astype(F32) * -rates)


def make_filters(tabs, rhs, ptable, w1, b1, w2, b2, w3, rates, hidden, filt, filt_spec, e_filt_spec, par):
    wave, _, _, e_wave, _, _ = tabs
    half, edge = wave.shape[1] // 3, e_wave.shape[1] // 6
    _, _, pre2 = hidden_layers(ptable[par], w1[...], b1[...], w2[...], b2[...])
    hidden[par] = jnp.sin(pre2)

    @pl.loop(0, 2)
    def _(o):
        filt[...] = fine_dot(hidden[par], w3[o])

        def fill(at):
            put_parts(rhs, at, 0, half, filt[at, :] * decay_at(par, CHUNK, at.start, rates[pl.ds(o, 1), :]))

        over_rows(half, CHUNK, fill)
        filt_spec[o, par] = dot(wave[...], rhs[0 : 3 * half, :]) * (1.0 / half)
        window = filt[pl.ds(0, edge), :] * decay_at(par, edge, 0, rates[pl.ds(o, 1), :])
        high, low = parts(jnp.concatenate([window, window], axis=0))
        e_filt_spec[o, par] = dot(e_wave[...], jnp.concatenate([high, low, high], axis=0)) * (1.0 / edge)


def turn_filters(tabs, filt_spec, e_filt_spec):
    wave, _, twist, e_wave, _, e_twist = tabs
    half, edge = wave.shape[1] // 3, e_wave.shape[1] // 6
    for o in range(2):
        def turn(at, o=o):
            real, imag = mul(*pair(filt_spec.at[o], 1, at, half), twist[at, 0:1], twist[at, 1:2])
            filt_spec[o, 2, at, :] = real
            filt_spec[o, 2, pl.ds(pl.multiple_of(at.start + half, 8), at.size), :] = imag

        over_rows(half, CHUNK, turn)
        n = 2 * edge
        real, imag = mul(*pair(e_filt_spec.at[o], 1, pl.ds(0, n), n), e_twist[:, 0:1], e_twist[:, 1:2])
        e_filt_spec[o, 2] = jnp.concatenate([real, imag], axis=0)


PAD = 8


def short_rows(z, which, par, at, masks, taps, tap_bias):
    size, start = at.size, at.start
    here = z[which, par, pl.ds(pl.multiple_of(start + PAD, 8), size), :]
    wide = pl.ds(pl.multiple_of(start, 8), size + PAD)
    same_before = z[which, par, wide, :][PAD - 1 : PAD - 1 + size]
    if par == 0:
        other = z[which, 1, wide, :][PAD - 1 : PAD - 1 + size]
    else:
        other = z[which, 0, pl.ds(pl.multiple_of(start + PAD, 8), size), :]
    one, two = masks[par, at, 3:4] * other, masks[par, at, 4:5] * same_before
    tap = lambda j: taps[j, which : which + 1, :]
    return tap_bias[which : which + 1, :] + tap(0) * here + tap(1) * one + tap(2) * two, here, one, two


def put_zpre(z, normed, weights, in_bias, which, par, half):
    zero = jnp.zeros((PAD, z.shape[3]), F32)
    z[which, par, 0:PAD, :] = zero
    z[which, par, PAD + half : PAD + half + PAD, :] = zero
    z[which, par, PAD : PAD + half, :] = dot(normed, weights) + in_bias[which : which + 1, :]


def make_short(short, z, masks, taps, tap_bias, half):
    for par in range(2):
        def work(at, par=par):
            for which in range(3):
                short[which, par, at, :] = short_rows(z, which, par, at, masks, taps, tap_bias)[0]

        over_rows(half, CHUNK, work)


def layer_norm_parts(values):
    center = jnp.mean(values, axis=-1, keepdims=True)
    centred = values - center
    spread = jnp.mean(centred * centred, axis=-1, keepdims=True)
    scale = lax.rsqrt(spread + EPSILON)
    return centred * scale, scale


def parity_matrix(rows):
    half = rows // 2
    at = lax.broadcasted_iota(jnp.int32, (rows, rows), 0)
    wanted = jnp.where(at < half, 2 * at, 2 * (at - half) + 1)
    return (lax.broadcasted_iota(jnp.int32, (rows, rows), 1) == wanted).astype(F32).astype(BF16)


def make_masks(masks, segments, half):
    seg = segments[...].astype(F32)
    length = seg.shape[1]
    place = lax.broadcasted_iota(jnp.int32, (1, length), 1)
    one = lambda ok: jnp.where(ok, 1.0, 0.0)
    rows = [one(seg == 1.0), one(seg == 0.0), one(seg == 2.0)]
    for j in (1, 2):
        rows.append(jnp.where(place >= j, one(pltpu.roll(seg, j, 1) == seg), 0.0))
    marks = jnp.concatenate(rows + [jnp.zeros((3, length), F32)], axis=0).astype(BF16)
    at = lax.broadcasted_iota(jnp.int32, (half, length), 0)
    column = lax.broadcasted_iota(jnp.int32, (half, length), 1)
    for par in range(2):
        choose = jnp.where(column == 2 * at + par, 1.0, 0.0).astype(BF16)
        masks[par, 0:half, :] = lax.dot_general(choose, marks, ROW_CONTRACT, preferred_element_type=F32)
        masks[par, half : half + PAD, :] = jnp.zeros((PAD, 8), F32)


def front(
    dp, tensor,
    tokens, cotangent, segments, gain, shift, in_shard, out_shard, up_shard, down_shard,
    b_in, taps, tap_bias, ptable, w1, b1, w2, b2, w3, rates, direct,
    wave, wave_back, twist, e_wave, e_back, e_twist,
    in_all, out_full, up_all, down_all, cot_full, norm_out, gated_out, own_gated, masks_out,
    z_out, filt_out, e_filt_out, spec_out, e_spec_out, conv_out, hidden_out,
    in_land, w_in, cot_own, norm_full, gated, masks, z, filt_spec, e_filt_spec, spec, e_spec, conv, hidden,
    short, rhs, rhs_even, rhs_odd, filt, send, recv, local,
):
    tabs = (wave, wave_back, twist, e_wave, e_back, e_twist)
    half = wave.shape[1] // 3
    count = tokens.shape[0]
    own = count // 2
    place = Place(dp, tensor)
    sems, copies = Sems(send, recv), LocalCopies(local)
    barrier = place.greet()

    parity = parity_matrix(count)
    normal, _ = layer_norm_parts(dot(parity, tokens[...]))
    low = (normal * gain[...] + shift[...]).astype(BF16)
    for par in range(2):
        norm_full[par, place.t] = low[par * own : (par + 1) * own]
    shuffled = dot(parity, cotangent[...]).astype(BF16)
    for par in range(2):
        cot_own[par] = shuffled[par * own : (par + 1) * own]
    place.met(barrier)

    norms = [
        tensor_gather(place, sems, norm_full.at[par, place.t], lambda i, par=par: norm_full.at[par, i]) for par in range(2)
    ]
    ins = dp_gather(place, sems, in_shard, lambda i: in_land.at[i])
    outs = dp_gather(place, sems, out_shard, lambda i: out_full.at[place.t, i])
    ups = dp_gather(place, sems, up_shard, lambda i: up_all.at[i])
    downs = dp_gather(place, sems, down_shard, lambda i: down_all.at[i])
    cots = [tensor_gather(place, sems, cot_own.at[par], lambda i, par=par: cot_full.at[par, i]) for par in range(2)]
    for gather in [*norms, ins, outs, ups, downs, *cots]:
        gather.start()
    own_in = copies.start(in_shard, in_land.at[place.d])
    own_out = copies.start(out_shard, out_full.at[place.t, place.d])
    copies.start(up_shard, up_all.at[place.d])
    copies.start(down_shard, down_all.at[place.d])
    for par in range(2):
        copies.start(cot_own.at[par], cot_full.at[par, place.t])

    make_masks(masks, segments, half)
    copies.start(masks, masks_out)
    net = (ptable, w1, b1, w2, b2, w3, rates, hidden, filt, filt_spec, e_filt_spec)
    make_filters(tabs, rhs, *net, 0)
    for gather in norms:
        gather.forward(tensor_origins(place))
    ins.forward(dp_origins(place))
    make_filters(tabs, rhs, *net, 1)
    turn_filters(tabs, filt_spec, e_filt_spec)
    copies.start(filt_spec, filt_out)
    copies.start(e_filt_spec, e_filt_out)
    copies.start(hidden, hidden_out)
    for gather in norms:
        gather.arrived()
    ins.arrived()
    copies.take(own_in)
    for which in range(3):
        w_in[which] = jnp.concatenate([in_land[i, which].astype(F32) for i in range(dp)], axis=0).astype(BF16)
    copies.start(in_land, in_all)
    copies.start(norm_full, norm_out)
    for par in range(2):
        normed = norm_full[par].reshape(half, -1)
        for which in range(3):
            put_zpre(z, normed, w_in[which], b_in, which, par, half)
    copies.start(z, z_out)
    for gather in cots:
        gather.forward(tensor_origins(place))
    outs.forward(dp_origins(place))
    make_short(short, z, masks, taps, tap_bias, half)

    def convolve(o, source):
        analyse(tabs, rhs, source, spec.at[o], e_spec.at[o], masks)
        copies.start(spec.at[o], spec_out.at[o])
        copies.start(e_spec.at[o], e_spec_out.at[o])
        edges = spectra_product(
            tabs, filt_spec.at[o], e_filt_spec.at[o], spec.at[o], e_spec.at[o], rhs_even, rhs_odd, False, False
        )
        synthesise(tabs, rhs_even, conv.at[o], 0)
        synthesise(tabs, rhs_odd, conv.at[o], 1)
        join(conv.at[o], edges, direct[o : o + 1, :], source, masks, half)
        copies.start(conv.at[o], conv_out.at[o])

    convolve(0, lambda par, at: short[0, par, at, :])
    outs.arrived()
    copies.take(own_out)
    out_rows = tensor_gather(place, sems, out_full.at[place.t], lambda i: out_full.at[i])
    out_rows.start()
    ups.forward(dp_origins(place))
    convolve(1, lambda par, at: short[1, par, at, :] * conv[0, par, at, :])
    out_rows.forward(tensor_origins(place))
    for par in range(2):
        for block in range(tensor):
            values = short[2, par, block * own : (block + 1) * own, :] * conv[1, par, block * own : (block + 1) * own, :]
            gated[par, block] = values.astype(BF16)
    trades = []
    for i in range(1, tensor):
        to = place.t_at(i)
        for par in range(2):
            trades.append(sems.copy(gated.at[par, to], own_gated.at[place.t, par], {"tensor": to}))
    for copy in trades:
        copy.start()
    for par in range(2):
        copies.start(gated.at[par, place.t], own_gated.at[place.t, par])
    copies.start(gated, gated_out)
    downs.forward(dp_origins(place))
    for gather in (*cots, ups, downs, out_rows):
        gather.arrived()
    for copy in trades:
        copy.wait()
    for gather in (*norms, ins, outs, ups, downs, *cots, out_rows):
        gather.finish()
    copies.finish()


def mixer_backward(
    d_mix, w_out, taps, tap_bias, ptable, w1, b1, w2, b2, w3, rates, direct, masks,
    wave, wave_back, twist, e_wave, e_back, e_twist,
    z, filt_spec, e_filt_spec, spec, e_spec, conv, hidden,
    d_z, g_in_bias, g_taps, g_tap_bias, g_direct, g_w1, g_b1, g_w2, g_b2, g_w3,
    short, rhs, rhs_even, rhs_odd, g, g_spec, e_g_spec, d_short, d_filt, acc,
):
    tabs = (wave, wave_back, twist, e_wave, e_back, e_twist)
    half = wave.shape[1] // 3
    width = z.shape[3]

    make_short(short, z, masks, taps, tap_bias, half)
    for par in range(2):
        g[par] = dot(d_mix[par], w_out[...])

        def gate(at, par=par):
            grad = g[par, at, :]
            d_short[2, par, pl.ds(pl.multiple_of(at.start, 8), at.size), :] = grad * conv[1, par, at, :]
            g[par, at, :] = grad * short[2, par, at, :]

        over_rows(half, CHUNK, gate)

    def back(o, forward_in, out):
        analyse(tabs, rhs, lambda par, at: g[par, at, :], g_spec, e_g_spec, masks)
        edges = spectra_product(
            tabs, filt_spec.at[o], e_filt_spec.at[o], g_spec, e_g_spec, rhs_even, rhs_odd, True, False
        )
        synthesise(tabs, rhs_even, out, 0)
        synthesise(tabs, rhs_odd, out, 1)
        join(out, edges, direct[o : o + 1, :], lambda par, at: g[par, at, :], masks, half)
        edges = spectra_product(tabs, spec.at[o], e_spec.at[o], g_spec, e_g_spec, rhs_even, rhs_odd, True, True)
        synthesise(tabs, rhs_even, d_filt.at[o], 0)
        synthesise(tabs, rhs_odd, d_filt.at[o], 1)
        acc[...] = jnp.zeros_like(acc)
        for par in range(2):
            edge = edges[par].shape[0] // 2

            def scale(at, par=par):
                d_filt[o, par, at, :] *= 1.0 / half
                acc[0:8, :] += jnp.sum((g[par, at, :] * forward_in(par, at)).reshape(-1, 8, width), axis=0)

            over_rows(half, CHUNK, scale)
            d_filt[o, par, 0:edge, :] += (edges[par][:edge] + edges[par][edge:]) * (1.0 / edge)
        g_direct[o : o + 1, :] = jnp.sum(acc[0:8, :], axis=0, keepdims=True)

    back(1, lambda par, at: short[1, par, at, :] * conv[0, par, at, :], d_short.at[0])
    for par in range(2):
        def gate(at, par=par):
            grad = d_short[0, par, at, :]
            d_short[1, par, at, :] = grad * conv[0, par, at, :]
            g[par, at, :] = grad * short[1, par, at, :]

        over_rows(half, CHUNK, gate)
    back(0, lambda par, at: short[0, par, at, :], d_short.at[0])

    for which in range(3):
        acc[...] = jnp.zeros_like(acc)
        for par in range(2):
            d_short[which, par, half : half + PAD, :] = jnp.zeros((PAD, width), F32)
        for par in range(2):
            def short_back(at, par=par, which=which):
                size, start = at.size, at.start
                tap = lambda j: taps[j, which : which + 1, :]
                _, here, one, two = short_rows(z, which, par, at, masks, taps, tap_bias)
                grad = d_short[which, par, at, :]
                fold = lambda x: jnp.sum(x.reshape(-1, 8, width), axis=0)
                acc[0:8, :] += fold(grad)
                acc[8:16, :] += fold(grad * here)
                acc[16:24, :] += fold(grad * one)
                acc[24:32, :] += fold(grad * two)
                wide = pl.ds(pl.multiple_of(start, 8), size + PAD)
                same = (d_short[which, par, wide, :] * masks[par, wide, 4:5])[1 : size + 1]
                if par == 0:
                    other = d_short[which, 1, at, :] * masks[1, at, 3:4]
                else:
                    other = (d_short[which, 0, wide, :] * masks[0, wide, 3:4])[1 : size + 1]
                low = (tap(0) * grad + tap(1) * other + tap(2) * same).astype(BF16)
                d_z[which, par, at, :] = low
                acc[32:40, :] += fold(low.astype(F32))

            over_rows(half, CHUNK, short_back)
        total = lambda i: jnp.sum(acc[8 * i : 8 * i + 8, :], axis=0, keepdims=True)
        g_tap_bias[which : which + 1, :] = total(0)
        for j in range(3):
            g_taps[j, which : which + 1, :] = total(1 + j)
        g_in_bias[which : which + 1, :] = total(4)

    for o in range(2):
        for par in range(2):
            def undo(at, par=par, o=o):
                d_filt[o, par, at, :] *= decay_at(par, CHUNK, at.start, rates[o : o + 1, :])

            over_rows(half, CHUNK, undo)
        g_w3[o] = fine_dot(hidden[0], d_filt[o, 0], COLUMN_CONTRACT) + fine_dot(hidden[1], d_filt[o, 1], COLUMN_CONTRACT)
    sums = None
    for par in range(2):
        pre1, h1, pre2 = hidden_layers(ptable[par], w1[...], b1[...], w2[...], b2[...])
        d_h2 = fine_dot(d_filt[0, par], w3[0], ROW_CONTRACT) + fine_dot(d_filt[1, par], w3[1], ROW_CONTRACT)
        d_pre2 = d_h2 * jnp.cos(pre2)
        d_h1 = fine_dot(d_pre2, w2[...], ROW_CONTRACT)
        d_pre1 = d_h1 * jnp.cos(pre1)
        own = (
            fine_dot(ptable[par], d_pre1, COLUMN_CONTRACT),
            jnp.sum(d_pre1, axis=0, keepdims=True),
            fine_dot(h1, d_pre2, COLUMN_CONTRACT),
            jnp.sum(d_pre2, axis=0, keepdims=True),
        )
        sums = own if sums is None else tuple(a + b for a, b in zip(sums, own, strict=True))
    g_w1[...], g_b1[...], g_w2[...], g_b2[...] = sums


MESH = pl.DeviceIdType.MESH


class Place:
    def __init__(self, dp, tensor):
        self.dp, self.tensor = dp, tensor
        self.rows = 4 if dp % 4 == 0 else 1
        self.cols = dp // self.rows
        self.cores = 2 if tensor % 2 == 0 else 1
        self.ys = tensor // self.cores
        self.d, self.t = lax.axis_index("dp"), lax.axis_index("tensor")
        self.a, self.b = self.d // self.cols, lax.rem(self.d, self.cols)
        self.y, self.c = self.t // self.cores, lax.rem(self.t, self.cores)

    def a_at(self, i):
        return lax.rem(self.a + i + self.rows, self.rows) * self.cols + self.b

    def b_at(self, i):
        return self.a * self.cols + lax.rem(self.b + i + self.cols, self.cols)

    def y_at(self, i):
        return lax.rem(self.y + i + self.ys, self.ys) * self.cores + self.c

    def core_peer(self):
        return self.y * self.cores + 1 - self.c

    def t_at(self, i):
        return lax.rem(self.t + i + self.tensor, self.tensor)

    def greet(self, dp=True, all_tensor=True):
        peers = [{"tensor": self.t_at(i)} for i in range(1, self.tensor)]
        if dp:
            peers += [{"dp": self.a_at(i)} for i in range(1, self.rows)]
            peers += [{"dp": self.b_at(i)} for i in range(1, self.cols)]
        barrier = pltpu.get_barrier_semaphore()
        for peer in peers:
            pl.semaphore_signal(barrier, inc=1, device_id=peer, device_id_type=MESH)
        self.expected = len(peers)
        return barrier

    def met(self, barrier):
        pl.semaphore_wait(barrier, self.expected)


class Sems:
    def __init__(self, send, recv):
        self.send, self.recv, self.used = send, recv, 0

    def copy(self, src, dst, device):
        i = self.used
        self.used += 1
        return pltpu.make_async_remote_copy(
            src_ref=src, dst_ref=dst, send_sem=self.send.at[i], recv_sem=self.recv.at[i],
            device_id=device, device_id_type=MESH,
        )


class LocalCopies:
    def __init__(self, sems):
        self.sems, self.open, self.used = sems, [], 0

    def start(self, src, dst):
        copy = pltpu.make_async_copy(src, dst, self.sems.at[self.used])
        self.used += 1
        copy.start()
        self.open.append(copy)
        return copy

    def take(self, copy):
        copy.wait()
        self.open = [other for other in self.open if other is not copy]

    def finish(self):
        for copy in self.open:
            copy.wait()


class Gather:
    def __init__(self, sems, source, slot, own, far, near, device):
        self.first = [sems.copy(source, slot(own), device(i)) for i in far]
        self.near = [sems.copy(source, slot(own), device(i)) for i in near]
        self.sems, self.slot, self.device, self.near_ids = sems, slot, device, near
        self.second = []

    def start(self):
        for copy in self.first + self.near:
            copy.start()

    def forward(self, origins, which=None):
        for i, origin in enumerate(origins):
            if which is not None and i not in which:
                continue
            self.first[i].wait_recv()
            for peer in self.near_ids:
                copy = self.sems.copy(self.slot(origin), self.slot(origin), self.device(peer))
                copy.start()
                self.second.append(copy)

    def arrived(self):
        for copy in self.near + self.second:
            copy.wait_recv()

    def finish(self):
        for copy in self.first + self.near + self.second:
            copy.wait_send()


def tensor_gather(place, sems, source, slot):
    near = [place.core_peer()] if place.cores == 2 else []
    return Gather(
        sems, source, slot, place.t, [place.y_at(i) for i in range(1, place.ys)], near, lambda i: {"tensor": i}
    )


def dp_gather(place, sems, source, slot):
    return Gather(
        sems, source, slot, place.d, [place.a_at(i) for i in range(1, place.rows)],
        [place.b_at(i) for i in range(1, place.cols)], lambda i: {"dp": i},
    )


def tensor_origins(place):
    return [place.y_at(-i) for i in range(1, place.ys)]


def dp_origins(place):
    return [place.a_at(-i) for i in range(1, place.rows)]


def gather_counts(dp, tensor):
    cores = 2 if tensor % 2 == 0 else 1
    rows = 4 if dp % 4 == 0 else 1
    far_t, near_t, far_d, near_d = tensor // cores - 1, cores - 1, rows - 1, dp // rows - 1
    return far_t + near_t + far_t * near_t, far_d + near_d + far_d * near_d


def vmem_specs(n):
    return [pl.BlockSpec(memory_space=pltpu.VMEM)] * n


def mix_shapes(half, width, hidden_width):
    edge4 = half // 4
    return dict(
        z=((3, 2, half + 2 * PAD, width), F32),
        filt_spec=((2, 3, 2 * half, width), F32),
        e_filt_spec=((2, 3, edge4, width), F32),
        spec=((2, 2, 2 * half, width), F32),
        e_spec=((2, 2, edge4, width), F32),
        conv=((2, 2, half, width), F32),
        hidden=((2, half, hidden_width), F32),
    )


def layer_norm(values, norm_gain, norm_shift):
    center = jnp.mean(values, axis=-1, keepdims=True)
    centred = values - center
    spread = jnp.mean(centred * centred, axis=-1, keepdims=True)
    return centred * lax.rsqrt(spread + EPSILON) * norm_gain + norm_shift


def smooth_gelu(values):
    return jax.nn.gelu(values, approximate=True)


def front_call(dp, tensor, args, count, model, channels, units, rows, half, hidden_width):
    S = jax.ShapeDtypeStruct
    own = count // 2
    shapes = mix_shapes(half, channels, hidden_width)
    land = ((dp, 3, rows, channels), BF16)
    norm, gate, mask = ((2, tensor, own, model), BF16), ((2, tensor, own, channels), BF16), ((2, half + PAD, 8), F32)
    outs = [
        S(*land), S((tensor, dp, rows, channels), BF16), S((dp, rows, units), BF16), S((dp, rows, units), BF16),
        S(*norm), S(*norm), S(*gate), S((tensor, 2, own, channels), BF16), S(*mask),
    ] + [S(*v) for v in shapes.values()]
    per_t, per_d = gather_counts(dp, tensor)
    copies = 5 * per_t + 4 * per_d + 2 * (tensor - 1)
    return pl.pallas_call(
        functools.partial(front, dp, tensor),
        out_shape=outs,
        in_specs=vmem_specs(5) + [pl.BlockSpec(memory_space=pl.ANY)] * 4 + vmem_specs(len(args) - 9),
        out_specs=[pl.BlockSpec(memory_space=pl.ANY)] * len(outs),
        scratch_shapes=[
            pltpu.VMEM(*land), pltpu.VMEM((3, model, channels), BF16), pltpu.VMEM((2, own, model), BF16),
            pltpu.VMEM(*norm), pltpu.VMEM(*gate), pltpu.VMEM(*mask),
        ] + [pltpu.VMEM(*v) for v in shapes.values()] + [
            pltpu.VMEM((3, 2, half, channels), F32),
            pltpu.VMEM((3 * half, channels), BF16),
            pltpu.VMEM((6 * half, channels), BF16),
            pltpu.VMEM((6 * half, channels), BF16),
            pltpu.VMEM((half, channels), F32),
            pltpu.SemaphoreType.DMA((copies,)),
            pltpu.SemaphoreType.DMA((copies,)),
            pltpu.SemaphoreType.DMA((24,)),
        ],
        compiler_params=pltpu.CompilerParams(collective_id=0, has_side_effects=True, vmem_limit_bytes=VMEM_LIMIT),
        name="front",
    )(*args)


def backward_call(args, half, width, emb, hidden_width):
    S = jax.ShapeDtypeStruct
    outs = [
        S((3, 2, half, width), BF16), S((3, width), F32), S((3, 3, width), F32), S((3, width), F32), S((2, width), F32),
        S((emb, hidden_width), F32), S((1, hidden_width), F32), S((hidden_width, hidden_width), F32), S((1, hidden_width), F32),
        S((2, hidden_width, width), F32),
    ]
    return pl.pallas_call(
        mixer_backward,
        out_shape=outs,
        in_specs=vmem_specs(len(args)),
        out_specs=vmem_specs(len(outs)),
        scratch_shapes=[
            pltpu.VMEM((3, 2, half, width), F32),
            pltpu.VMEM((3 * half, width), BF16),
            pltpu.VMEM((6 * half, width), BF16),
            pltpu.VMEM((6 * half, width), BF16),
            pltpu.VMEM((2, half, width), F32),
            pltpu.VMEM((2, 2 * half, width), F32),
            pltpu.VMEM((2, half // 4, width), F32),
            pltpu.VMEM((3, 2, half + PAD, width), F32),
            pltpu.VMEM((2, 2, half, width), F32),
            pltpu.VMEM((40, width), F32),
        ],
        compiler_params=pltpu.CompilerParams(vmem_limit_bytes=VMEM_LIMIT),
        name="mixer_backward",
    )(*args)


def smooth_gelu(values):
    return jax.nn.gelu(values, approximate=True)


def body(
    tokens,
    segment_ids,
    mix_norm_gain,
    mix_norm_bias,
    in_weight,
    in_bias,
    short_weight,
    short_bias,
    filt_in_weight,
    filt_in_bias,
    filt_mid_weight,
    filt_mid_bias,
    filt_out_weight,
    decay_rates,
    long_bias,
    out_weight,
    out_bias,
    mlp_norm_gain,
    mlp_norm_bias,
    up_weight,
    up_bias,
    down_weight,
    down_bias,
    cotangent,
):
    residual = tokens[0].astype(jnp.float32)
    doc_ids = segment_ids[0]
    model_width = residual.shape[1]
    length = doc_ids.shape[0]
    dp, tensor = lax.axis_size("dp"), lax.axis_size("tensor")
    rows, channels, units, count = in_weight.shape[0], in_weight.shape[2], up_weight.shape[1], tokens.shape[1]
    half, hidden_width = length // 2, filt_mid_bias.shape[0]

    def take_rows(weight_flat, incoming):
        product = jnp.dot(incoming, weight_flat, preferred_element_type=jnp.float32)
        return (product, incoming)

    def back_rows(weight_all, kept_low, incoming):
        product = jnp.dot(incoming, weight_all, preferred_element_type=jnp.float32)
        weight_grad = lax.dot_general(
            incoming, kept_low, COLUMN_CONTRACT, preferred_element_type=jnp.float32
        )
        return (product, weight_grad)

    def sum_terms(left_low, weight_all):
        return lax.dot_general(
            left_low, weight_all, ROW_CONTRACT, preferred_element_type=jnp.float32
        )

    normed, first_norm_back = jax.vjp(layer_norm, residual, mix_norm_gain, mix_norm_bias)
    normed_low = normed.astype(jnp.bfloat16)
    tables = tuple(jnp.asarray(t) for t in wave_tables(length))
    ptable = jnp.asarray(position_table(length, filt_in_weight.shape[0]))
    net = (
        short_weight, short_bias, ptable, filt_in_weight, filt_in_bias[None], filt_mid_weight,
        filt_mid_bias[None], jnp.swapaxes(filt_out_weight, 0, 1), decay_rates, long_bias,
    )
    in_par, out_par, up_par, down_par, cot_par, norm_par, gated_par, own_gated, masks, *kept = front_call(
        dp, tensor,
        (tokens[0], cotangent[0], segment_ids, mix_norm_gain[None], mix_norm_bias[None], jnp.swapaxes(in_weight, 0, 1), out_weight,
         up_weight, down_weight, in_bias) + net + tables,
        count, model_width, channels, units, rows, half, hidden_width,
    )
    in_flat = jnp.swapaxes(in_par, 1, 2).reshape(model_width, 3 * channels)
    out_full = jnp.moveaxis(out_par.reshape(tensor, model_width, channels), 0, 1).reshape(model_width, model_width)
    out_all = lax.dynamic_index_in_dim(out_par, lax.axis_index("tensor"), 0, False).reshape(model_width, channels)
    up_all, down_all = up_par.reshape(model_width, units), down_par.reshape(model_width, units)
    normed_full = in_order(norm_par.reshape(2, half, model_width))
    cot_full = in_order(cot_par.reshape(2, half, model_width))
    gated_low = in_order(gated_par.reshape(2, half, channels))
    own_gated = in_order(jnp.moveaxis(own_gated, 0, 2).reshape(2, count // 2, model_width))
    mixed = lax.dot_general(own_gated, out_full, ROW_CONTRACT, preferred_element_type=jnp.float32)
    mixed_sum = residual + mixed + out_bias
    normed_two, second_norm_back = jax.vjp(layer_norm, mixed_sum, mlp_norm_gain, mlp_norm_bias)
    normed_two_low = normed_two.astype(jnp.bfloat16)
    up_raw, normed_two_full = take_rows(
        up_all, lax.all_gather(normed_two_low, "tensor", axis=0, tiled=True)
    )
    pre_act = up_raw + up_bias
    activated, gelu_back = jax.vjp(smooth_gelu, pre_act)
    act_low = activated.astype(jnp.bfloat16)
    mlp_sum = lax.psum_scatter(
        sum_terms(act_low, down_all), "tensor", scatter_dimension=0, tiled=True
    )
    output = (mixed_sum + mlp_sum + down_bias).astype(jnp.bfloat16)
    grad_low = cotangent[0]
    grad_out = grad_low.astype(jnp.float32)
    grad_down_bias = jnp.sum(grad_out, axis=0)
    d_act, grad_down = back_rows(
        down_all, act_low, cot_full
    )
    d_pre_low = gelu_back(d_act)[0].astype(jnp.bfloat16)
    grad_up_bias = jnp.sum(d_pre_low, axis=0, dtype=jnp.float32)
    grad_up = lax.dot_general(
        normed_two_full, d_pre_low, COLUMN_CONTRACT, preferred_element_type=jnp.float32
    )
    d_normed_two = lax.psum_scatter(
        sum_terms(d_pre_low, up_all), "tensor", scatter_dimension=0, tiled=True
    )
    d_mixed_norm, grad_mlp_gain, grad_mlp_shift = second_norm_back(d_normed_two)
    d_mixed = grad_out + d_mixed_norm
    grad_out_bias = jnp.sum(d_mixed, axis=0)
    d_mix_low = d_mixed.astype(jnp.bfloat16)
    d_mix_full = lax.all_gather(d_mix_low, "tensor", axis=0, tiled=True)
    grad_out_w = lax.dot_general(d_mix_full, gated_low, COLUMN_CONTRACT, preferred_element_type=jnp.float32)
    (
        d_z_par, grad_in_bias, grad_taps, grad_tap_bias, grad_direct, grad_first_w, grad_first_b, grad_middle_w, grad_middle_b,
        grad_last_w,
    ) = backward_call((by_parity(d_mix_full), out_all) + net + (masks,) + tables + tuple(kept), half, channels, filt_in_weight.shape[0], hidden_width)
    grad_first_b, grad_middle_b = grad_first_b[0], grad_middle_b[0]
    grad_last_w = jnp.swapaxes(grad_last_w, 0, 1)
    d_z_low = in_order(jnp.moveaxis(d_z_par, 0, 2)).reshape(length, 3 * channels)
    grad_in = lax.dot_general(
        normed_full, d_z_low, COLUMN_CONTRACT, preferred_element_type=jnp.float32
    ).reshape(model_width, 3, channels)
    d_normed = lax.psum_scatter(
        sum_terms(d_z_low, in_flat), "tensor", scatter_dimension=0, tiled=True
    )
    d_input_norm, grad_mix_gain, grad_mix_shift = first_norm_back(d_normed)
    grad_tokens = (d_mixed + d_input_norm).astype(jnp.bfloat16)[None]
    grad_in, grad_out_w, grad_up, grad_down = (
        lax.psum_scatter(grad_in, "dp", scatter_dimension=0, tiled=True),
        lax.psum_scatter(grad_out_w, "dp", scatter_dimension=0, tiled=True),
        lax.psum_scatter(grad_up, "dp", scatter_dimension=0, tiled=True),
        lax.psum_scatter(grad_down, "dp", scatter_dimension=0, tiled=True),
    )
    grad_in_bias, grad_taps, grad_tap_bias, grad_last_w, grad_direct, grad_up_bias = lax.psum(
        (grad_in_bias, grad_taps, grad_tap_bias, grad_last_w, grad_direct, grad_up_bias), "dp"
    )
    (
        grad_mix_gain,
        grad_mix_shift,
        grad_first_w,
        grad_first_b,
        grad_middle_w,
        grad_middle_b,
        grad_out_bias,
        grad_mlp_gain,
        grad_mlp_shift,
        grad_down_bias,
    ) = lax.psum(
        (
            grad_mix_gain,
            grad_mix_shift,
            grad_first_w,
            grad_first_b,
            grad_middle_w,
            grad_middle_b,
            grad_out_bias,
            grad_mlp_gain,
            grad_mlp_shift,
            grad_down_bias,
        ),
        ("dp", "tensor"),
    )
    return (
        output[None],
        grad_tokens,
        grad_mix_gain,
        grad_mix_shift,
        grad_in,
        grad_in_bias,
        grad_taps,
        grad_tap_bias,
        grad_first_w,
        grad_first_b,
        grad_middle_w,
        grad_middle_b,
        grad_last_w,
        grad_direct,
        grad_out_w,
        grad_out_bias,
        grad_mlp_gain,
        grad_mlp_shift,
        grad_up,
        grad_up_bias,
        grad_down,
        grad_down_bias,
    )


def solution(mesh):
    placed = (
        P("dp", "tensor", None),
        P("dp", None),
        P(),
        P(),
        P("dp", None, "tensor"),
        P(None, "tensor"),
        P(None, None, "tensor"),
        P(None, "tensor"),
        P(),
        P(),
        P(),
        P(),
        P(None, None, "tensor"),
        P(None, "tensor"),
        P(None, "tensor"),
        P("dp", "tensor"),
        P(),
        P(),
        P(),
        P("dp", "tensor"),
        P("tensor"),
        P("dp", "tensor"),
        P(),
        P("dp", "tensor", None),
    )
    return jax.shard_map(
        body,
        mesh=mesh,
        in_specs=placed,
        out_specs=(
            P("dp", "tensor", None),
            P("dp", "tensor", None),
            P(),
            P(),
            P("dp", None, "tensor"),
            P(None, "tensor"),
            P(None, None, "tensor"),
            P(None, "tensor"),
            P(),
            P(),
            P(),
            P(),
            P(None, None, "tensor"),
            P(None, "tensor"),
            P("dp", "tensor"),
            P(),
            P(),
            P(),
            P("dp", "tensor"),
            P("tensor"),
            P("dp", "tensor"),
            P(),
        ),
        check_vma=False,
    )
```

time: 1350 us -> 685 us (0.51)
  other arithmetic: 316 us -> 10.5 us
  matrix products: 300 us -> 35.6 us
  local copies, waits for them, and re-layouts: 185 us -> 42.3 us
  Pallas kernels: 0 us -> 116 us
  blocking collectives: 134 us -> 71.7 us
  starting transfers between devices: 16.2 us -> 0.67 us
    dot_general x32 -> x1, matrix products: 250 us -> 1.5 us  [body(): lax.dot_general(d_mix_full, gated_low, COLUMN_CONTRACT, preferred_element...]
    pallas_call x0 -> x2, Pallas kernels: none -> 116 us  [the longest x1 62.3 us: front_call(): pl.pallas_call(functools.partial(front, dp, tensor), out_shape=outs, in_s...]
    reduce_sum x10 -> x0, other arithmetic: 105 us -> none  [the longest x2 64.2 us: long_conv(): spec_imag * filt_imag]
    reduce_scatter x0 -> x1, waiting for transfers between devices: none -> 72.1 us  [body(): lax.psum_scatter(grad_down, 'dp', scatter_dimension=0, tiled=True)]
    unnamed x16 -> x10, waiting for transfers between devices: 71 us -> 0.16 us
    dot_general x10 -> x1, local copies, waits for them, and re-layouts: 66.8 us -> 1.44 us  [body(): lax.dot_general(normed_full, d_z_low, COLUMN_CONTRACT, preferred_element_...]
    all_gather x6 -> x1, waiting for transfers between devices: 75.9 us -> 15.8 us  [body(): d_mix_full = lax.all_gather(d_mix_low, 'tensor', axis=0, tiled=True)]
    add_any x13 -> x0, other arithmetic: 57.8 us -> none  [the longest x2 25.1 us: long_conv(): spec_real = spectrum[:, :size_b]]
  transfers between devices with their start and end apart: 16 -> 10, of which waited for: 10 -> 10; matrix products, arithmetic and copies ran while one was open for 35% -> 8% of each run, Pallas kernels for 0% -> 0%
where the time goes in v1:
time: 685 us; the launch traced here: 680 us
  waiting for transfers between devices  388 us (57%)
  Pallas kernels  116 us (17%)
  blocking collectives  71.7 us (10%)
  local copies, waits for them, and re-layouts  42.3 us (6%)
  matrix products  35.6 us (5%)
  between operations  15 us (2%)
  other arithmetic  10.5 us (2%)
    reduce_scatter x1, waiting for transfers between devices, body(): lax.psum_scatter(grad_in, 'dp', scatter_dimension=0, tiled=True)  73 us
    reduce_scatter x1, waiting for transfers between devices, body(): lax.psum_scatter(grad_down, 'dp', scatter_dimension=0, tiled=True)  72.1 us
    reduce_scatter x1, waiting for transfers between devices, body(): lax.psum_scatter(grad_out_w, 'dp', scatter_dimension=0, tiled=True)  64.8 us
    pallas_call x1, Pallas kernels, front_call(): pl.pallas_call(functools.partial(front, dp, tensor), out_shape=outs, in_s...  62.3 us
    pallas_call x1, Pallas kernels, backward_call(): pl.pallas_call(mixer_backward, out_shape=outs, in_specs=vmem_specs(len(ar...  53.3 us
    psum x1, blocking collectives, body(): lax.psum((grad_mix_gain, grad_mix_shift, grad_first_w, grad_first_b, grad...  41.2 us
    reduce_scatter x1, waiting for transfers between devices, body(): lax.psum_scatter(sum_terms(d_z_low, in_flat), 'tensor', scatter_dimension...  39.9 us
    reduce_scatter x1, waiting for transfers between devices, body(): lax.psum_scatter(sum_terms(act_low, down_all), 'tensor', scatter_dimensio...  39.2 us
  transfers between devices with their start and end apart: 10, of which 10 were waited for; matrix products, arithmetic and copies ran while one was open for 8% of the time, Pallas kernels for 0%

profile of v1, /device:TPU:1, one launch (start us, length us, event | category | flops | bytes accessed | tf_op | source)
XLA Modules:
  0.0 679.5 jit_solution(14853103337798116357)
XLA Ops:
  11.3 62.3 %front.1 = (bf16[8,3,96,192]{3,2,1,0:T(8,128)(2,1)}, bf16[4,8,96,192]{3,2,1,0:T(8,128)(2,1)}, bf16[8,96,768]{2,1,0:T(8,128)(2,1)}, bf16[8,96,768]{2,1,0:T(8,128)...) custom-call(bf16[256,768]{1,0:T(8,128)(2,1)} %bitcast.87, ...), custom_call_target="tpu_custom_call" | custom-call | tf_op jit(solution)/shard_map/front/pallas_call | solution.py:699
  76.0 1.7 copy.72
  79.6 3.0 copy.91
  84.1 24.0 %all-gather.3.cloned.1.call-done = bf16[1024,768]{1,0:T(8,128)(2,1)} async-done(((bf16[256,768]{1,0:T(8,128)(2,1)}), bf16[1024,768]{1,0:T(8,128)(2,1)}) %all-gather.3.cloned.1.call-update) | async-done | bytes 1572880 | tf_op jit(solution)/shard_map/all_gather | solution.py:832
  108.1 3.3 fusion.31
  111.4 3.7 convert_reduce_fusion
  116.3 3.1 fusion.32
  119.5 5.7 fusion.26
  125.2 31.9 %reduce-scatter.10.cloned.1.call-done = f32[256,768]{1,0:T(8,128)} async-done(((f32[1024,768]{1,0:T(8,128)}), f32[256,768]{1,0:T(8,128)}) %reduce-scatter.10.cloned.1.call-update) | async-done | bytes 786448 | tf_op jit(solution)/shard_map/reduce_scatter | solution.py:852
  158.6 39.2 %reduce-scatter.8.cloned.1.call-done = f32[256,768]{1,0:T(8,128)} async-done(((f32[1024,768]{1,0:T(8,128)}), f32[256,768]{1,0:T(8,128)}) %reduce-scatter.8.cloned.1.call-update) | async-done | bytes 786448 | tf_op jit(solution)/shard_map/reduce_scatter | solution.py:837
  197.8 2.4 fusion.29
  202.1 1.6 copy.76
  204.7 1.8 constant_dynamic-slice_fusion
  206.5 15.8 %all-gather.5.cloned.1.call-done = bf16[1024,768]{1,0:T(8,128)(2,1)} async-done(((bf16[256,768]{1,0:T(8,128)(2,1)}), bf16[1024,768]{1,0:T(8,128)(2,1)}) %all-gather.5.cloned.1.call-update) | async-done | bytes 1572880 | tf_op jit(solution)/shard_map/all_gather | solution.py:859
  222.3 3.5 reshape.166
  227.2 53.3 %mixer_backward.1 = (bf16[3,2,512,192]{3,2,1,0:T(8,128)(2,1)}, f32[3,192]{1,0:T(4,128)}, f32[3,3,192]{2,1,0:T(4,128)}, f32[3,192]{1,0:T(4,128)}, f32[2,192]{1,0:...) custom-call(bf16[2,512,768]{2,1,0:T(8,128)(2,1)} %bitcast.90, ...), custom_call_target="tpu_custom_call" | custom-call | tf_op jit(solution)/shard_map/mixer_backward/pallas_call | solution.py:729
  280.6 2.8 copy.75
  283.3 2.7 reshape_reshape.3
  286.0 4.4 fusion.33
  291.8 4.3 fusion.35
  297.5 4.9 fusion.25
  306.1 3.0 copy.89
  309.1 1.6 reshape.170
  312.4 4.2 fusion.7
  317.3 30.5 %all-reduce.1 = (f32[3,192]{1,0:T(4,128)}, f32[3,3,192]{2,1,0:T(4,128)}, f32[3,192]{1,0:T(4,128)}, f32[2,192]{1,0:T(2,128)}, f32[768]{0:T(1024)}) all-reduce(f32[3,192]{1,0:T(4,128)S(1)} %copy-done.20, f32[3,3,192]{2,1,0:T(4,128)S(1)} %copy-done.17, f32[3,192]{1,0:T(4,128)S(1)} %copy-done.21, ...), channel_id=1, replica_groups=mesh['dp'=8,'tensor'=4] {'dp'}, use_global_device_ids=true, to_apply=%region_16.17 | all-reduce | flops 4032 | bytes 32256 | tf_op jit(solution)/shard_map/psum | solution.py:882
  348.2 1.7 copy.81
  349.9 39.9 %reduce-scatter.12.cloned.1.call-done = f32[256,768]{1,0:T(8,128)} async-done(((f32[1024,768]{1,0:T(8,128)}), f32[256,768]{1,0:T(8,128)}) %reduce-scatter.12.cloned.1.call-update) | async-done | bytes 786448 | tf_op jit(solution)/shard_map/reduce_scatter | solution.py:871
  394.2 41.2 %all-reduce = (f32[768]{0:T(1024)}, f32[768]{0:T(1024)}, f32[33,64]{1,0:T(8,128)}, f32[64]{0:T(128)}, f32[64,64]{1,0:T(8,128)}, /*index=5*/f32[64]{0:T(128)}, f3...) all-reduce(f32[768]{0:T(1024)S(1)} %get-tuple-element.142, ...), channel_id=1, replica_groups=mesh['dp'=8,'tensor'=4] {'dp','tensor'}, use_global_device_ids=true, to_apply=%region_12.13 | all-reduce | flops 10944 | bytes 87552 | tf_op jit(solution)/shard_map/psum | solution.py:896
  435.4 27.0 %reduce-scatter.18.cloned.1.call-done = f32[96,768]{1,0:T(8,128)} async-done(((f32[768,768]{1,0:T(8,128)}), f32[96,768]{1,0:T(8,128)}) %reduce-scatter.18.cloned.1.call-update) | async-done | bytes 294928 | tf_op jit(solution)/shard_map/reduce_scatter | solution.py:879
  462.3 72.1 %reduce-scatter.20.cloned.1.call-done = f32[96,768]{1,0:T(8,128)} async-done(((f32[768,768]{1,0:T(8,128)}), f32[96,768]{1,0:T(8,128)}) %reduce-scatter.20.cloned.1.call-update) | async-done | bytes 294928 | tf_op jit(solution)/shard_map/reduce_scatter | solution.py:880
  534.5 64.8 %reduce-scatter.16.cloned.1.call-done = f32[96,192]{1,0:T(8,128)} async-done(((f32[768,192]{1,0:T(8,128)}), f32[96,192]{1,0:T(8,128)}) %reduce-scatter.16.cloned.1.call-update) | async-done | bytes 73744 | tf_op jit(solution)/shard_map/reduce_scatter | solution.py:878
  599.2 73.0 %reduce-scatter.14.cloned.1.call-done = f32[96,3,192]{2,0,1:T(8,128)} async-done(((f32[768,3,192]{2,0,1:T(8,128)}), f32[96,3,192]{2,0,1:T(8,128)}) %reduce-scatter.14.cloned.1.call-update) | async-done | bytes 221200 | tf_op jit(solution)/shard_map/reduce_scatter | solution.py:877
  (114 shorter events, 30.4 us)
Async XLA Ops:
  7.2 100.9 %all-gather.3.cloned.1.call-start = ((), (), s32[]{:S(2)}) async-start(), calls=%async_computation.7 | async-start | bytes 1966080 | tf_op jit(solution)/shard_map/all_gather | solution.py:832
  75.0 2.8 copy-start
  75.0 2.8 copy-start.18
  79.5 77.6 %reduce-scatter.10.cloned.1.call-start = ((), (), s32[]{:S(2)}) async-start(), calls=%async_computation.9 | async-start | bytes 3932160 | tf_op jit(solution)/shard_map/reduce_scatter | solution.py:852
  108.1 3.3 copy-start.7
  108.1 3.3 copy-start.27
  108.1 3.3 copy-start.29
  111.4 3.8 copy-start.30
  111.4 4.9 copy-start.28
  119.5 78.4 %reduce-scatter.8.cloned.1.call-start = ((), (), s32[]{:S(2)}) async-start(), calls=%async_computation.8 | async-start | bytes 3932160 | tf_op jit(solution)/shard_map/reduce_scatter | solution.py:837
  125.2 72.7 %copy-start.22 = (f32[768]{0:T(1024)S(1)}, f32[768]{0:T(1024)}, u32[]{:S(2)}) copy-start(f32[768]{0:T(1024)} %param.53) | copy-start | bytes 9220
  125.2 75.9 %copy-start.5 = (bf16[1,256,768]{2,1,0:T(8,128)(2,1)S(1)}, bf16[1,256,768]{2,1,0:T(8,128)(2,1)}, u32[]{:S(2)}) copy-start(bf16[1,256,768]{2,1,0:T(8,128)(2,1)} %param.54) | copy-start | bytes 1179652
  125.2 97.1 %all-gather.5.cloned.1.call-start = ((), (), s32[]{:S(2)}) async-start(), calls=%async_computation.10 | async-start | bytes 1966080 | tf_op jit(solution)/shard_map/all_gather | solution.py:859
  158.6 43.5 %copy-start.11 = (bf16[8,3,96,192]{3,2,1,0:T(8,128)(2,1)S(1)}, bf16[8,3,96,192]{3,2,1,0:T(8,128)(2,1)}, u32[]{:S(2)}) copy-start(bf16[8,3,96,192]{3,2,1,0:T(8,128)(2,1)} %get-tuple-element.62) | copy-start | bytes 2654212
  202.1 146.1 %all-reduce.4.cloned.1.call-start = ((), (), s32[]{:S(2)}) async-start(), calls=%async_computation.13 | async-start | bytes 262144 | tf_op jit(solution)/shard_map/psum | solution.py:882
  280.5 109.2 %reduce-scatter.12.cloned.1.call-start = ((), (), s32[]{:S(2)}) async-start(), calls=%async_computation.11 | async-start | bytes 3932160 | tf_op jit(solution)/shard_map/reduce_scatter | solution.py:871
  290.4 1.4 copy-start.26
  290.4 171.9 %reduce-scatter.18.cloned.1.call-start = ((), (), s32[]{:S(2)}) async-start(), calls=%async_computation.15 | async-start | bytes 2654208 | tf_op jit(solution)/shard_map/reduce_scatter | solution.py:879
  296.1 238.3 %reduce-scatter.20.cloned.1.call-start = ((), (), s32[]{:S(2)}) async-start(), calls=%async_computation.16 | async-start | bytes 2654208 | tf_op jit(solution)/shard_map/reduce_scatter | solution.py:880
  302.4 2.1 copy-start.9
  302.4 296.8 %reduce-scatter.16.cloned.1.call-start = ((), (), s32[]{:S(2)}) async-start(), calls=%async_computation.14 | async-start | bytes 884736 | tf_op jit(solution)/shard_map/reduce_scatter | solution.py:878
  306.0 366.2 %reduce-scatter.14.cloned.1.call-start = ((), (), s32[]{:S(2)}) async-start(), calls=%async_computation.12 | async-start | bytes 2654208 | tf_op jit(solution)/shard_map/reduce_scatter | solution.py:877
  309.1 1.6 copy-start.4
  310.7 1.7 copy-start.10
  316.5 73.2 %copy-start.13 = (f32[768]{0:T(1024)S(1)}, f32[768]{0:T(1024)}, u32[]{:S(2)}) copy-start(f32[768]{0:T(1024)} %param.33) | copy-start | bytes 9220
  316.5 76.4 %copy-start.2 = (f32[256,768]{1,0:T(8,128)S(1)}, f32[256,768]{1,0:T(8,128)}, u32[]{:S(2)}) copy-start(f32[256,768]{1,0:T(8,128)} %copy-done.1) | copy-start | bytes 2359300
  316.6 76.4 %copy-start.6 = (bf16[1,256,768]{2,1,0:T(8,128)(2,1)S(1)}, bf16[1,256,768]{2,1,0:T(8,128)(2,1)}, u32[]{:S(2)}) copy-start(bf16[1,256,768]{2,1,0:T(8,128)(2,1)} %param.54) | copy-start | bytes 1179652
  349.9 44.3 %copy-start.15 = (f32[64,64]{1,0:T(8,128)S(1)}, f32[64,64]{1,0:T(8,128)}, u32[]{:S(2)}) copy-start(f32[64,64]{1,0:T(8,128)} %get-tuple-element.69) | copy-start | bytes 49156
  349.9 44.3 %copy-start.16 = (f32[33,64]{1,0:T(8,128)S(1)}, f32[33,64]{1,0:T(8,128)}, u32[]{:S(2)}) copy-start(f32[33,64]{1,0:T(8,128)} %get-tuple-element.67) | copy-start | bytes 25348
  349.9 44.3 %copy-start.24 = (f32[1,64]{1,0:T(1,128)S(1)}, f32[1,64]{1,0:T(1,128)}, u32[]{:S(2)}) copy-start(f32[1,64]{1,0:T(1,128)} %get-tuple-element.68) | copy-start | bytes 772
  349.9 44.3 %copy-start.25 = (f32[1,64]{1,0:T(1,128)S(1)}, f32[1,64]{1,0:T(1,128)}, u32[]{:S(2)}) copy-start(f32[1,64]{1,0:T(1,128)} %get-tuple-element.70) | copy-start | bytes 772
  389.8 3.2 copy-start.3
  (10 other events, 9.1 us)
Sparse Core Ops, SparseCore 0:
  79.7 28.3 all-gather.2
  119.6 37.5 reduce-scatter.9
  159.9 37.9 reduce-scatter.7
  202.2 20.0 all-gather.4
  280.6 67.5 all-reduce.3
  350.8 38.9 reduce-scatter.11
  393.8 68.4 reduce-scatter.17
  466.4 68.0 reduce-scatter.19
  538.3 60.8 reduce-scatter.15
  603.5 68.6 reduce-scatter.13

commit v2 on v1

--- a/solution.py
+++ b/solution.py
@@ -295,7 +295,7 @@
     tokens, cotangent, segments, gain, shift, in_shard, out_shard, up_shard, down_shard,
     b_in, taps, tap_bias, ptable, w1, b1, w2, b2, w3, rates, direct,
     wave, wave_back, twist, e_wave, e_back, e_twist,
-    in_all, out_full, up_all, down_all, cot_full, norm_out, gated_out, own_gated, masks_out,
+    w_in_out, out_full, up_all, down_all, cot_full, norm_out, gated_out, own_gated, masks_out,
     z_out, filt_out, e_filt_out, spec_out, e_spec_out, conv_out, hidden_out,
     in_land, w_in, cot_own, norm_full, gated, masks, z, filt_spec, e_filt_spec, spec, e_spec, conv, hidden,
     short, rhs, rhs_even, rhs_odd, filt, send, recv, local,
@@ -353,7 +353,7 @@
     copies.take(own_in)
     for which in range(3):
         w_in[which] = jnp.concatenate([in_land[i, which].astype(F32) for i in range(dp)], axis=0).astype(BF16)
-    copies.start(in_land, in_all)
+    copies.start(w_in, w_in_out)
     copies.start(norm_full, norm_out)
     for par in range(2):
         normed = norm_full[par].reshape(half, -1)
@@ -409,117 +409,6 @@
     copies.finish()
 
 
-def mixer_backward(
-    d_mix, w_out, taps, tap_bias, ptable, w1, b1, w2, b2, w3, rates, direct, masks,
-    wave, wave_back, twist, e_wave, e_back, e_twist,
-    z, filt_spec, e_filt_spec, spec, e_spec, conv, hidden,
-    d_z, g_in_bias, g_taps, g_tap_bias, g_direct, g_w1, g_b1, g_w2, g_b2, g_w3,
-    short, rhs, rhs_even, rhs_odd, g, g_spec, e_g_spec, d_short, d_filt, acc,
-):
-    tabs = (wave, wave_back, twist, e_wave, e_back, e_twist)
-    half = wave.shape[1] // 3
-    width = z.shape[3]
-
-    make_short(short, z, masks, taps, tap_bias, half)
-    for par in range(2):
-        g[par] = dot(d_mix[par], w_out[...])
-
-        def gate(at, par=par):
-            grad = g[par, at, :]
-            d_short[2, par, pl.ds(pl.multiple_of(at.start, 8), at.size), :] = grad * conv[1, par, at, :]
-            g[par, at, :] = grad * short[2, par, at, :]
-
-        over_rows(half, CHUNK, gate)
-
-    def back(o, forward_in, out):
-        analyse(tabs, rhs, lambda par, at: g[par, at, :], g_spec, e_g_spec, masks)
-        edges = spectra_product(
-            tabs, filt_spec.at[o], e_filt_spec.at[o], g_spec, e_g_spec, rhs_even, rhs_odd, True, False
-        )
-        synthesise(tabs, rhs_even, out, 0)
-        synthesise(tabs, rhs_odd, out, 1)
-        join(out, edges, direct[o : o + 1, :], lambda par, at: g[par, at, :], masks, half)
-        edges = spectra_product(tabs, spec.at[o], e_spec.at[o], g_spec, e_g_spec, rhs_even, rhs_odd, True, True)
-        synthesise(tabs, rhs_even, d_filt.at[o], 0)
-        synthesise(tabs, rhs_odd, d_filt.at[o], 1)
-        acc[...] = jnp.zeros_like(acc)
-        for par in range(2):
-            edge = edges[par].shape[0] // 2
-
-            def scale(at, par=par):
-                d_filt[o, par, at, :] *= 1.0 / half
-                acc[0:8, :] += jnp.sum((g[par, at, :] * forward_in(par, at)).reshape(-1, 8, width), axis=0)
-
-            over_rows(half, CHUNK, scale)
-            d_filt[o, par, 0:edge, :] += (edges[par][:edge] + edges[par][edge:]) * (1.0 / edge)
-        g_direct[o : o + 1, :] = jnp.sum(acc[0:8, :], axis=0, keepdims=True)
-
-    back(1, lambda par, at: short[1, par, at, :] * conv[0, par, at, :], d_short.at[0])
-    for par in range(2):
-        def gate(at, par=par):
-            grad = d_short[0, par, at, :]
-            d_short[1, par, at, :] = grad * conv[0, par, at, :]
-            g[par, at, :] = grad * short[1, par, at, :]
-
-        over_rows(half, CHUNK, gate)
-    back(0, lambda par, at: short[0, par, at, :], d_short.at[0])
-
-    for which in range(3):
-        acc[...] = jnp.zeros_like(acc)
-        for par in range(2):
-            d_short[which, par, half : half + PAD, :] = jnp.zeros((PAD, width), F32)
-        for par in range(2):
-            def short_back(at, par=par, which=which):
-                size, start = at.size, at.start
-                tap = lambda j: taps[j, which : which + 1, :]
-                _, here, one, two = short_rows(z, which, par, at, masks, taps, tap_bias)
-                grad = d_short[which, par, at, :]
-                fold = lambda x: jnp.sum(x.reshape(-1, 8, width), axis=0)
-                acc[0:8, :] += fold(grad)
-                acc[8:16, :] += fold(grad * here)
-                acc[16:24, :] += fold(grad * one)
-                acc[24:32, :] += fold(grad * two)
-                wide = pl.ds(pl.multiple_of(start, 8), size + PAD)
-                same = (d_short[which, par, wide, :] * masks[par, wide, 4:5])[1 : size + 1]
-                if par == 0:
-                    other = d_short[which, 1, at, :] * masks[1, at, 3:4]
-                else:
-                    other = (d_short[which, 0, wide, :] * masks[0, wide, 3:4])[1 : size + 1]
-                low = (tap(0) * grad + tap(1) * other + tap(2) * same).astype(BF16)
-                d_z[which, par, at, :] = low
-                acc[32:40, :] += fold(low.astype(F32))
-
-            over_rows(half, CHUNK, short_back)
-        total = lambda i: jnp.sum(acc[8 * i : 8 * i + 8, :], axis=0, keepdims=True)
-        g_tap_bias[which : which + 1, :] = total(0)
-        for j in range(3):
-            g_taps[j, which : which + 1, :] = total(1 + j)
-        g_in_bias[which : which + 1, :] = total(4)
-
-    for o in range(2):
-        for par in range(2):
-            def undo(at, par=par, o=o):
-                d_filt[o, par, at, :] *= decay_at(par, CHUNK, at.start, rates[o : o + 1, :])
-
-            over_rows(half, CHUNK, undo)
-        g_w3[o] = fine_dot(hidden[0], d_filt[o, 0], COLUMN_CONTRACT) + fine_dot(hidden[1], d_filt[o, 1], COLUMN_CONTRACT)
-    sums = None
-    for par in range(2):
-        pre1, h1, pre2 = hidden_layers(ptable[par], w1[...], b1[...], w2[...], b2[...])
-        d_h2 = fine_dot(d_filt[0, par], w3[0], ROW_CONTRACT) + fine_dot(d_filt[1, par], w3[1], ROW_CONTRACT)
-        d_pre2 = d_h2 * jnp.cos(pre2)
-        d_h1 = fine_dot(d_pre2, w2[...], ROW_CONTRACT)
-        d_pre1 = d_h1 * jnp.cos(pre1)
-        own = (
-            fine_dot(ptable[par], d_pre1, COLUMN_CONTRACT),
-            jnp.sum(d_pre1, axis=0, keepdims=True),
-            fine_dot(h1, d_pre2, COLUMN_CONTRACT),
-            jnp.sum(d_pre2, axis=0, keepdims=True),
-        )
-        sums = own if sums is None else tuple(a + b for a, b in zip(sums, own, strict=True))
-    g_w1[...], g_b1[...], g_w2[...], g_b2[...] = sums
-
-
 MESH = pl.DeviceIdType.MESH
 
 
@@ -549,9 +438,14 @@
     def t_at(self, i):
         return lax.rem(self.t + i + self.tensor, self.tensor)
 
-    def greet(self, dp=True, all_tensor=True):
+    def d_at(self, i):
+        return lax.rem(self.d + i + self.dp, self.dp)
+
+    def greet(self, dp=True, all_dp=False):
         peers = [{"tensor": self.t_at(i)} for i in range(1, self.tensor)]
-        if dp:
+        if all_dp:
+            peers += [{"dp": self.d_at(i)} for i in range(1, self.dp)]
+        elif dp:
             peers += [{"dp": self.a_at(i)} for i in range(1, self.rows)]
             peers += [{"dp": self.b_at(i)} for i in range(1, self.cols)]
         barrier = pltpu.get_barrier_semaphore()
@@ -660,28 +554,17 @@
     return [pl.BlockSpec(memory_space=pltpu.VMEM)] * n
 
 
-def mix_shapes(half, width, hidden_width):
+def mix_shapes(half, width, hidden_width, filter_parts=3):
     edge4 = half // 4
     return dict(
         z=((3, 2, half + 2 * PAD, width), F32),
-        filt_spec=((2, 3, 2 * half, width), F32),
-        e_filt_spec=((2, 3, edge4, width), F32),
+        filt_spec=((2, filter_parts, 2 * half, width), F32),
+        e_filt_spec=((2, filter_parts, edge4, width), F32),
         spec=((2, 2, 2 * half, width), F32),
         e_spec=((2, 2, edge4, width), F32),
         conv=((2, 2, half, width), F32),
         hidden=((2, half, hidden_width), F32),
     )
-
-
-def layer_norm(values, norm_gain, norm_shift):
-    center = jnp.mean(values, axis=-1, keepdims=True)
-    centred = values - center
-    spread = jnp.mean(centred * centred, axis=-1, keepdims=True)
-    return centred * lax.rsqrt(spread + EPSILON) * norm_gain + norm_shift
-
-
-def smooth_gelu(values):
-    return jax.nn.gelu(values, approximate=True)
 
 
 def front_call(dp, tensor, args, count, model, channels, units, rows, half, hidden_width):
@@ -691,7 +574,7 @@
     land = ((dp, 3, rows, channels), BF16)
     norm, gate, mask = ((2, tensor, own, model), BF16), ((2, tensor, own, channels), BF16), ((2, half + PAD, 8), F32)
     outs = [
-        S(*land), S((tensor, dp, rows, channels), BF16), S((dp, rows, units), BF16), S((dp, rows, units), BF16),
+        S((3, model, channels), BF16), S((tensor, dp, rows, channels), BF16), S((dp, rows, units), BF16), S((dp, rows, units), BF16),
         S(*norm), S(*norm), S(*gate), S((tensor, 2, own, channels), BF16), S(*mask),
     ] + [S(*v) for v in shapes.values()]
     per_t, per_d = gather_counts(dp, tensor)
@@ -719,37 +602,702 @@
     )(*args)
 
 
-def backward_call(args, half, width, emb, hidden_width):
+class Reduce:
+    def __init__(self, place, sems, near_out, near_in, far_out, far_in):
+        self.place, self.near_in, self.near_out, self.far_in, self.far_out = place, near_in, near_out, far_in, far_out
+        peer = {"tensor": place.core_peer()}
+        self.near = [sems.copy(near_out.at[i], near_in.at[i], peer) for i in range(place.ys)] if place.cores == 2 else []
+        self.far = []
+        if far_in is not None:
+            self.far = [
+                sems.copy(far_out.at[i - 1], far_in.at[i - 1], {"tensor": place.y_at(i)}) for i in range(1, place.ys)
+            ]
+
+    def order(self):
+        place = self.place
+        blocks = []
+        for i in [0] + list(range(place.ys - 1, 0, -1)):
+            for other in range(place.cores):
+                owner = place.y_at(i)
+                blocks.append((i, other, owner + (1 - 2 * place.c) if other else owner))
+        return blocks
+
+    def combine(self, keep, rows, send=True):
+        for i in list(range(1, self.place.ys)) + [0]:
+            if self.near:
+                self.near[i].wait_recv()
+
+            def work(at, i=i):
+                total = keep[i, at, :]
+                if self.near:
+                    total = total + self.near_in[i, at, :].astype(F32)
+                if i:
+                    self.far_out[i - 1, at, :] = total.astype(BF16)
+                else:
+                    keep[0, at, :] = total
+
+            over_rows(rows, 32, work)
+            if i and send:
+                self.far[i - 1].start()
+
+    def total(self, keep, at):
+        out = keep[0, at, :]
+        for i in range(self.place.ys - 1):
+            out = out + self.far_in[i, at, :].astype(F32)
+        return out
+
+    def arrived(self):
+        for copy in self.far:
+            copy.wait_recv()
+
+    def finish(self):
+        for copy in self.near + self.far:
+            copy.wait_send()
+
+
+GELU_SCALE = math.sqrt(2.0 / math.pi)
+
+
+def gelu_and_slope(x):
+    square = x * x
+    bent = jnp.tanh(GELU_SCALE * (x + 0.044715 * (x * square)))
+    slope = 0.5 * (1.0 + bent) + 0.5 * x * (1.0 - bent * bent) * (GELU_SCALE + (3.0 * 0.044715 * GELU_SCALE) * square)
+    return 0.5 * x * (1.0 + bent), slope
+
+
+def fold8(x):
+    return jnp.sum(x.reshape(-1, 8, x.shape[1]), axis=0)
+
+
+def norm_back(grad, normal, scale, gain):
+    k = grad * gain
+    return scale * (k - jnp.mean(k, axis=-1, keepdims=True) - normal * jnp.mean(k * normal, axis=-1, keepdims=True))
+
+
+def put_weight_grad(place, grad, left, right, low):
+    rows = low.shape[2]
+
+    @pl.loop(0, 2)
+    def _(par):
+        flat = lambda ref: ref[par].reshape(-1, ref.shape[-1])
+        part = lax.dot_general(flat(left), flat(right), COLUMN_CONTRACT, preferred_element_type=F32)
+
+        @pl.when(par == 0)
+        def _():
+            grad[...] = part
+
+        @pl.when(par != 0)
+        def _():
+            grad[...] += part
+
+    for a in range(place.rows):
+        for b in range(place.cols):
+            start = (a * place.cols + b) * rows
+            low[b, a] = grad[start : start + rows, :].astype(BF16)
+
+
+def middle(
+    dp, tensor,
+    tokens, cotangent, own_gated, out_full, out_bias, gain, shift, up_all, up_bias, down_all, cot_full,
+    down_bias,
+    d_mixed_out, d_mix_low, mlp_own, mlp_far, g_down, g_up, row_sums, up_sums,
+    mixed, normal, scales, norm_full, d_act, pre, acts, d_pres, keep, near_out, near_in, far_out, far_in, keep_mlp, near_out_mlp, near_in_mlp,
+    far_mlp, cot_rows, grad, low_down, low_up, acc, up_acc,
+    send, recv, local,
+):
+    count, model = tokens.shape
+    own, units = count // 2, up_all.shape[1]
+    place = Place(dp, tensor)
+    sems, copies = Sems(send, recv), LocalCopies(local)
+    barrier = place.greet(dp=False)
+    parity = parity_matrix(count)
+    residual = dot(parity, tokens[...])
+    total = residual + out_bias[...]
+    for block in range(tensor):
+        rows = jnp.concatenate([own_gated[block, 0], own_gated[block, 1]], axis=0)
+        total += lax.dot_general(rows, out_full[block], ROW_CONTRACT, preferred_element_type=F32)
+    mixed[...] = total
+    xhat, scale = layer_norm_parts(total)
+    normal[...] = xhat
+    scales[...] = jnp.broadcast_to(scale, scales.shape)
+    low = (xhat * gain[...] + shift[...]).astype(BF16)
+    for par in range(2):
+        norm_full[par, place.t] = low[par * own : (par + 1) * own]
+    place.met(barrier)
+    gathers = [
+        tensor_gather(place, sems, norm_full.at[par, place.t], lambda i, par=par: norm_full.at[par, i]) for par in range(2)
+    ]
+    for gather in gathers:
+        gather.start()
+    reduce = Reduce(place, sems, near_out, near_in, far_out, far_in)
+    up_acc[...] = jnp.zeros_like(up_acc)
+
+    def block_rows(ref, owner):
+        return jnp.concatenate([ref[0, owner], ref[1, owner]], axis=0)
+
+    @pl.loop(0, tensor)
+    def _(block):
+        d_act[block] = dot(jnp.concatenate([cot_full[0, block], cot_full[1, block]], axis=0), down_all[...])
+
+    def work_block(step, other, owner):
+        pre[...] = dot(block_rows(norm_full, owner), up_all[...]) + up_bias[...]
+
+        for par in range(2):
+            def work(at, par=par):
+                rows = pl.ds(pl.multiple_of(par * own + at.start, 16), at.size)
+                act, slope = gelu_and_slope(pre[rows, :])
+                acts[par, owner, at, :] = act.astype(BF16)
+                d_pre = (d_act[owner, rows, :] * slope).astype(BF16)
+                d_pres[par, owner, at, :] = d_pre
+                up_acc[...] += fold8(d_pre.astype(F32))
+
+            over_rows(own, 16, work)
+        part = lax.dot_general(block_rows(d_pres, owner), up_all[...], ROW_CONTRACT, preferred_element_type=F32)
+        if other:
+            near_out[step] = part.astype(BF16)
+            reduce.near[step].start()
+        else:
+            keep[step] = part
+
+    blocks = reduce.order()
+    forwarded = False
+    for step, other, owner in blocks:
+        if step == 0 and other:
+            for gather in gathers:
+                for copy in gather.near:
+                    copy.wait_recv()
+        if step and not forwarded:
+            for gather in gathers:
+                gather.forward(tensor_origins(place))
+            forwarded = True
+        if step and other:
+            for gather in gathers:
+                gather.second[place.ys - 1 - step].wait_recv()
+        work_block(step, other, owner)
+    reduce.combine(keep, count)
+    sums = Reduce(place, sems, near_out_mlp, near_in_mlp, far_mlp, None)
+    for step, other, owner in blocks[::-1]:
+        part = lax.dot_general(block_rows(acts, owner), down_all[...], ROW_CONTRACT, preferred_element_type=F32)
+        if other:
+            near_out_mlp[step] = part.astype(BF16)
+            sums.near[step].start()
+        else:
+            keep_mlp[step] = part
+    put_weight_grad(place, grad, cot_full, acts, low_down)
+    copies.start(low_down, g_down)
+    put_weight_grad(place, grad, norm_full, d_pres, low_up)
+    copies.start(low_up, g_up)
+    sums.combine(keep_mlp, count, send=False)
+    if place.ys > 1:
+        copies.start(far_mlp, mlp_far)
+
+    def own_rows(at):
+        mlp_own[at, :] = keep_mlp[0, at, :] + mixed[at, :] + down_bias[...]
+
+    over_rows(count, 32, own_rows)
+    up_sums[...] = jnp.sum(up_acc[...], axis=0, keepdims=True)
+    for gather in gathers:
+        gather.finish()
+    acc[...] = jnp.zeros_like(acc)
+    cot_rows[...] = dot(parity, cotangent[...])
+    reduce.arrived()
+
+    def back(at):
+        grad = reduce.total(keep, at)
+        xhat = normal[at, :]
+        out_grad = cot_rows[at, :]
+        d_mixed = out_grad + norm_back(grad, xhat, scales[at, 0:1], gain[...])
+        mixed[at, :] = d_mixed
+        d_mix_low[at, :] = d_mixed.astype(BF16)
+        acc[0:8, :] += fold8(grad * xhat)
+        acc[8:16, :] += fold8(grad)
+        acc[16:24, :] += fold8(d_mixed)
+        acc[24:32, :] += fold8(out_grad)
+
+    over_rows(count, 16, back)
+    copies.start(mixed, d_mixed_out)
+    for i in range(4):
+        row_sums[i : i + 1, :] = jnp.sum(acc[8 * i : 8 * i + 8, :], axis=0, keepdims=True)
+    reduce.finish()
+    sums.finish()
+    copies.finish()
+
+
+def middle_call(dp, tensor, args):
     S = jax.ShapeDtypeStruct
-    outs = [
-        S((3, 2, half, width), BF16), S((3, width), F32), S((3, 3, width), F32), S((3, width), F32), S((2, width), F32),
-        S((emb, hidden_width), F32), S((1, hidden_width), F32), S((hidden_width, hidden_width), F32), S((1, hidden_width), F32),
-        S((2, hidden_width, width), F32),
+    count, model = args[0].shape
+    units = args[7].shape[1]
+    own, cores, rows_d = count // 2, 2 if tensor % 2 == 0 else 1, 4 if dp % 4 == 0 else 1
+    ys, farther = tensor // cores, max(tensor // cores - 1, 1)
+    rows, low_rows = ((count, model), F32), ((ys, count, model), BF16)
+    blocks, norms = ((2, tensor, own, units), BF16), ((2, tensor, own, model), BF16)
+    low_grad = ((dp // rows_d, rows_d, model // dp, units), BF16)
+    far = ((farther, count, model), BF16)
+    per_t, _ = gather_counts(dp, tensor)
+    total = 2 * per_t + 3 * ys
+    hbm, vmem = pl.BlockSpec(memory_space=pl.ANY), pl.BlockSpec(memory_space=pltpu.VMEM)
+    return pl.pallas_call(
+        functools.partial(middle, dp, tensor),
+        out_shape=[
+            S(*rows), S((count, model), BF16), S(*rows), S(*far), S(*low_grad), S(*low_grad), S((4, model), F32), S((1, units), F32),
+        ],
+        in_specs=vmem_specs(len(args)),
+        out_specs=[hbm, vmem, vmem, hbm, hbm, hbm, vmem, vmem],
+        scratch_shapes=[
+            pltpu.VMEM(*rows), pltpu.VMEM(*rows), pltpu.VMEM((count, 128), F32), pltpu.VMEM(*norms),
+            pltpu.VMEM((tensor, count, units), F32), pltpu.VMEM((count, units), F32),
+            pltpu.VMEM(*blocks), pltpu.VMEM(*blocks), pltpu.VMEM((ys, count, model), F32),
+            pltpu.VMEM(*low_rows), pltpu.VMEM(*low_rows), pltpu.VMEM(*far), pltpu.VMEM(*far),
+            pltpu.VMEM((ys, count, model), F32), pltpu.VMEM(*low_rows), pltpu.VMEM(*low_rows), pltpu.VMEM(*far),
+            pltpu.VMEM(*rows), pltpu.VMEM((model, units), F32), pltpu.VMEM(*low_grad), pltpu.VMEM(*low_grad),
+            pltpu.VMEM((32, model), F32), pltpu.VMEM((8, units), F32),
+            pltpu.SemaphoreType.DMA((total,)), pltpu.SemaphoreType.DMA((total,)), pltpu.SemaphoreType.DMA((8,)),
+        ],
+        compiler_params=pltpu.CompilerParams(collective_id=1, has_side_effects=True, vmem_limit_bytes=VMEM_LIMIT),
+        name="middle",
+    )(*args)
+
+
+class WeightReduce:
+    def __init__(self, place, sems, low, near_in, keep, far_out, far_in):
+        self.place, self.low, self.near_in, self.keep, self.far_out, self.far_in = place, low, near_in, keep, far_out, far_in
+        own = lambda i: lax.rem(place.b + i, place.cols)
+        self.near = [
+            sems.copy(low.at[own(i)], near_in.at[i - 1], {"dp": place.b_at(i)}) for i in range(1, place.cols)
+        ]
+        self.far = [sems.copy(far_out.at[i - 1], far_in.at[i - 1], {"dp": place.a_at(i)}) for i in range(1, place.rows)]
+
+    def start(self):
+        for copy in self.near:
+            copy.start()
+
+    def combine(self, own_blocks=None):
+        place = self.place
+        for copy in self.near:
+            copy.wait_recv()
+        for i in list(range(1, place.rows)) + [0]:
+            a = lax.rem(place.a + i, place.rows)
+            total = (self.low[place.b, a] if own_blocks is None else own_blocks[a]).astype(F32)
+            for j in range(place.cols - 1):
+                total = total + self.near_in[j, a].astype(F32)
+            if i:
+                self.far_out[i - 1] = total.astype(BF16)
+                self.far[i - 1].start()
+            else:
+                self.keep[...] = total
+
+    def total(self):
+        for copy in self.far:
+            copy.wait_recv()
+        out = self.keep[...]
+        for i in range(self.place.rows - 1):
+            out = out + self.far_in[i].astype(F32)
+        return out
+
+    def finish(self):
+        for copy in self.near + self.far:
+            copy.wait_send()
+
+
+def order_matrix(rows):
+    half = rows // 2
+    at = lax.broadcasted_iota(jnp.int32, (rows, rows), 0)
+    wanted = lax.rem(at, 2) * half + at // 2
+    return (lax.broadcasted_iota(jnp.int32, (rows, rows), 1) == wanted).astype(F32).astype(BF16)
+
+
+MISC, TAPS, FIRST, SECOND, BIASES = 0, 8, 24, 64, 128
+
+
+def rear(
+    dp, tensor,
+    tokens, d_mix_low, row_sums, up_sums, gain, taps, tap_bias, ptable, w1, b1, w2, b2, w3, rates, direct,
+    d_mixed_in, mlp_own, mlp_far, g_down, g_up, norm_in, gated_in, w_in_in, out_in, masks_in,
+    wave_in, wave_back_in, twist, e_wave, e_back, e_twist,
+    z_in, filt_in, e_filt_in, spec_in, e_spec_in, conv_in, hidden_in,
+    output, grad_tokens, o_down, o_up, o_in, o_out, o_small, o_first, o_rows,
+    wave, wave_back, masks, z, filt_spec, e_filt_spec, spec, e_spec, conv, hidden,
+    d_mixed, norm_full, gated, w_in, w_out, d_mix_full, mlp_in, own_down, own_up,
+    short, rhs_even, rhs_odd, g, g_spec, e_g_spec, d_short, d_z, acc, normal, scales,
+    down_near, down_keep, down_far, down_land, up_near, up_keep, up_far, up_land,
+    in_low, in_near, in_keep, in_far, in_land, out_low, out_near, out_keep, out_far, out_land,
+    keep, near_out, near_in, far_out, far_in,
+    small, small_in, small_own, small_all, first, first_in, sums, sums_in, wide, wide_in,
+    send, recv, local,
+):
+    tabs = (wave, wave_back, twist, e_wave, e_back, e_twist)
+    half, width = z.shape[2] - 2 * PAD, z.shape[3]
+    count, model = tokens.shape
+    own = count // 2
+    d_filt, rhs = conv, rhs_even
+    place = Place(dp, tensor)
+    sems, copies = Sems(send, recv), LocalCopies(local)
+    barrier = place.greet(all_dp=True)
+    loads = {}
+    for name, src, dst in (
+        ("z", z_in, z), ("masks", masks_in, masks), ("out", out_in.at[place.t], w_out), ("conv", conv_in, conv),
+        ("gated", gated_in, gated), ("wave", wave_in, wave), ("norm", norm_in, norm_full), ("filt", filt_in.at[:, 0:2], filt_spec),
+        ("e_filt", e_filt_in.at[:, 0:2], e_filt_spec), ("wave_back", wave_back_in, wave_back), ("down", g_down.at[place.b], own_down),
+        ("up", g_up.at[place.b], own_up), ("spec", spec_in, spec), ("e_spec", e_spec_in, e_spec), ("w_in", w_in_in, w_in),
+        ("mixed", d_mixed_in, d_mixed), ("hidden", hidden_in, hidden),
+    ):
+        loads[name] = copies.start(src, dst)
+
+    def loaded(*names):
+        for name in names:
+            copies.take(loads[name])
+
+    for par in range(2):
+        d_mix_full[par, place.t] = d_mix_low[par * own : (par + 1) * own, :]
+    place.met(barrier)
+    gathers = [
+        tensor_gather(place, sems, d_mix_full.at[par, place.t], lambda i, par=par: d_mix_full.at[par, i]) for par in range(2)
     ]
+    for gather in gathers:
+        gather.start()
+    downs = WeightReduce(place, sems, g_down, down_near, down_keep, down_far, down_land)
+    ups = WeightReduce(place, sems, g_up, up_near, up_keep, up_far, up_land)
+    ins = [
+        WeightReduce(place, sems, in_low.at[p], in_near.at[p], in_keep.at[p], in_far.at[p], in_land.at[p]) for p in range(3)
+    ]
+    outs = WeightReduce(place, sems, out_low, out_near, out_keep, out_far, out_land)
+    downs.start()
+    ups.start()
+    mlp = [sems.copy(mlp_far.at[i - 1], mlp_in.at[i - 1], {"tensor": place.y_at(i)}) for i in range(1, place.ys)]
+    for copy in mlp:
+        copy.start()
+
+    xhat, scale = layer_norm_parts(dot(parity_matrix(count), tokens[...]))
+    normal[...] = xhat
+    scales[...] = jnp.broadcast_to(scale, scales.shape)
+    loaded("z", "masks")
+    make_short(short, z, masks, taps, tap_bias, half)
+    loaded("out", "conv")
+    for gather in gathers:
+        gather.forward(tensor_origins(place))
+    for gather in gathers:
+        gather.arrived()
+    for par in range(2):
+        g[par] = dot(d_mix_full[par].reshape(half, model), w_out[...])
+
+        def gate(at, par=par):
+            grad = g[par, at, :]
+            d_short[2, par, at, :] = grad * conv[1, par, at, :]
+            g[par, at, :] = grad * short[2, par, at, :]
+
+        over_rows(half, CHUNK, gate)
+
+    rows = model // dp
+
+    def weight_blocks(low, total):
+        for a in range(place.rows):
+            for b in range(place.cols):
+                start = (a * place.cols + b) * rows
+                low[b, a] = total[start : start + rows, :].astype(BF16)
+
+    def in_grad(p):
+        total = None
+        for par in range(2):
+            part = lax.dot_general(
+                norm_full[par].reshape(half, model), d_z[p, par], COLUMN_CONTRACT, preferred_element_type=F32
+            )
+            total = part if total is None else total + part
+        weight_blocks(in_low.at[p], total)
+        ins[p].start()
+
+    base = 2 * w3.shape[1]
+
+    def short_back_all(which):
+        acc[...] = jnp.zeros_like(acc)
+        for par in range(2):
+            d_short[which, par, half : half + PAD, :] = jnp.zeros((PAD, width), F32)
+        for par in range(2):
+            def work(at, par=par):
+                size, start = at.size, at.start
+                tap = lambda j: taps[j, which : which + 1, :]
+                _, here, one, two = short_rows(z, which, par, at, masks, taps, tap_bias)
+                grad = d_short[which, par, at, :]
+                acc[0:8, :] += fold8(grad)
+                acc[8:16, :] += fold8(grad * here)
+                acc[16:24, :] += fold8(grad * one)
+                acc[24:32, :] += fold8(grad * two)
+                rows_on = pl.ds(pl.multiple_of(start, 8), size + PAD)
+                same = (d_short[which, par, rows_on, :] * masks[par, rows_on, 4:5])[1 : size + 1]
+                if par == 0:
+                    other = d_short[which, 1, at, :] * masks[1, at, 3:4]
+                else:
+                    other = (d_short[which, 0, rows_on, :] * masks[0, rows_on, 3:4])[1 : size + 1]
+                low = (tap(0) * grad + tap(1) * other + tap(2) * same).astype(BF16)
+                d_z[which, par, at, :] = low
+                acc[32:40, :] += fold8(low.astype(F32))
+
+            over_rows(half, CHUNK, work)
+        total = lambda i: jnp.sum(acc[8 * i : 8 * i + 8, :], axis=0, keepdims=True)
+        small[pl.ds(base + MISC + which, 1), :] = total(4)
+        small[pl.ds(base + MISC + 3 + which, 1), :] = total(0)
+        for j in range(3):
+            small[pl.ds(base + TAPS + 3 * j + which, 1), :] = total(1 + j)
+
+    small[...] = jnp.zeros_like(small)
+    loaded("gated")
+    total = None
+    for par in range(2):
+        part = lax.dot_general(
+            d_mix_full[par].reshape(half, model), gated[par].reshape(half, width), COLUMN_CONTRACT, preferred_element_type=F32
+        )
+        total = part if total is None else total + part
+    weight_blocks(out_low, total)
+    outs.start()
+    loaded("wave")
+
+    def spread_back(o, out):
+        analyse(tabs, rhs, lambda par, at: g[par, at, :], g_spec, e_g_spec, masks)
+        if o:
+            loaded("filt", "e_filt", "wave_back")
+        edges = spectra_product(
+            tabs, filt_spec.at[o], e_filt_spec.at[o], g_spec, e_g_spec, rhs_even, rhs_odd, True, True
+        )
+        synthesise(tabs, rhs_even, out, 0)
+        synthesise(tabs, rhs_odd, out, 1)
+        join(out, edges, direct[o : o + 1, :], lambda par, at: g[par, at, :], masks, half)
+
+    def filter_back(o, forward_in):
+        edges = spectra_product(tabs, spec.at[o], e_spec.at[o], g_spec, e_g_spec, rhs_even, rhs_odd, True, True)
+        synthesise(tabs, rhs_even, d_filt.at[o], 0)
+        synthesise(tabs, rhs_odd, d_filt.at[o], 1)
+        acc[...] = jnp.zeros_like(acc)
+        for par in range(2):
+            edge = edges[par].shape[0] // 2
+            d_filt[o, par, 0:edge, :] += (edges[par][:edge] + edges[par][edge:]) * (half / edge)
+
+            def work(at, par=par):
+                decay = decay_at(par, CHUNK, at.start, rates[o : o + 1, :])
+                d_filt[o, par, at, :] = d_filt[o, par, at, :] * (decay * (1.0 / half))
+                acc[0:8, :] += fold8(g[par, at, :] * forward_in(par, at))
+
+            over_rows(half, CHUNK, work)
+        small[pl.ds(base + MISC + 6 + o, 1), :] = jnp.sum(acc[0:8, :], axis=0, keepdims=True)
+
+    spread_back(1, d_short.at[0])
+    short_back_all(2)
+    loaded("norm")
+    in_grad(2)
+    loaded("down")
+    downs.combine(own_down)
+    loaded("spec", "e_spec")
+    filter_back(1, lambda par, at: short[1, par, at, :] * conv[0, par, at, :])
+    for par in range(2):
+        def gate_again(at, par=par):
+            grad = d_short[0, par, at, :]
+            d_short[1, par, at, :] = grad * conv[0, par, at, :]
+            g[par, at, :] = grad * short[1, par, at, :]
+
+        over_rows(half, CHUNK, gate_again)
+    loaded("up")
+    ups.combine(own_up)
+    spread_back(0, d_short.at[0])
+    short_back_all(1)
+    in_grad(1)
+    outs.combine()
+    ins[2].combine()
+    short_back_all(0)
+    loaded("w_in")
+    reduce = Reduce(place, sems, near_out, near_in, far_out, far_in)
+    for step, other, owner in reduce.order()[::-1]:
+        at = pl.ds(pl.multiple_of(owner * own, 16), own)
+        part = None
+        for p in range(3):
+            rows_p = jnp.concatenate([d_z[p, 0, at, :], d_z[p, 1, at, :]], axis=0)
+            term = lax.dot_general(rows_p, w_in[p], ROW_CONTRACT, preferred_element_type=F32)
+            part = term if part is None else part + term
+        if other:
+            near_out[step] = part.astype(BF16)
+            reduce.near[step].start()
+        else:
+            keep[step] = part
+    in_grad(0)
+    reduce.combine(keep, count)
+    ins[1].combine()
+
+    filter_back(0, lambda par, at: short[0, par, at, :])
+    loaded("hidden")
+    hidden_width = w3.shape[1]
+    for o in range(2):
+        small[o * hidden_width : (o + 1) * hidden_width, :] = fine_dot(
+            hidden[0], d_filt[o, 0], COLUMN_CONTRACT
+        ) + fine_dot(hidden[1], d_filt[o, 1], COLUMN_CONTRACT)
+    first[...] = jnp.zeros_like(first)
+    emb = w1.shape[0]
+    f_second, f_bias = 40, 40 + hidden_width
+    for par in range(2):
+        pre1, h1, pre2 = hidden_layers(ptable[par], w1[...], b1[...], w2[...], b2[...])
+        d_h2 = fine_dot(d_filt[0, par], w3[0], ROW_CONTRACT) + fine_dot(d_filt[1, par], w3[1], ROW_CONTRACT)
+        d_pre2 = d_h2 * jnp.cos(pre2)
+        d_h1 = fine_dot(d_pre2, w2[...], ROW_CONTRACT)
+        d_pre1 = d_h1 * jnp.cos(pre1)
+        first[0:emb, :] += fine_dot(ptable[par], d_pre1, COLUMN_CONTRACT)
+        first[f_second:f_bias, :] += fine_dot(h1, d_pre2, COLUMN_CONTRACT)
+        first[f_bias : f_bias + 1, :] += jnp.sum(d_pre1, axis=0, keepdims=True)
+        first[f_bias + 1 : f_bias + 2, :] += jnp.sum(d_pre2, axis=0, keepdims=True)
+    trades = [sems.copy(first, first_in.at[i - 1], {"tensor": place.t_at(i)}) for i in range(1, tensor)]
+    for copy in trades:
+        copy.start()
+    ins[0].combine()
+
+    sums[...] = jnp.zeros_like(sums)
+    loaded("mixed")
+    wide[...] = jnp.zeros_like(wide)
+    reduce.arrived()
+
+    def back(at):
+        grad = reduce.total(keep, at)
+        hat = normal[at, :]
+        d_input = norm_back(grad, hat, scales[at, 0:1], gain[...])
+        near_out[0, at, :] = (d_mixed[at, :] + d_input).astype(BF16)
+        wide[0:8, 0:model] += fold8(grad * hat)
+        wide[8:16, 0:model] += fold8(grad)
+
+    reduce.finish()
+    over_rows(count, 16, back)
+    mlp_sum = d_mixed
+    mlp_loaded = copies.start(mlp_own, mlp_sum)
+    sums[0:1, :] = jnp.sum(wide[0:8, 0:model], axis=0, keepdims=True)
+    sums[1:2, :] = jnp.sum(wide[8:16, 0:model], axis=0, keepdims=True)
+    sums[2:6, :] = row_sums[...]
+    row_trades = [sems.copy(sums, sums_in.at[i - 1], {"tensor": place.t_at(i)}) for i in range(1, tensor)]
+    for copy in row_trades:
+        copy.start()
+
+    for copy in trades:
+        copy.wait_recv()
+    total = first[...]
+    for i in range(tensor - 1):
+        total = total + first_in[i]
+    small[base + FIRST : base + FIRST + emb, 0:hidden_width] = total[0:emb]
+    small[base + SECOND : base + SECOND + hidden_width, 0:hidden_width] = total[f_second:f_bias]
+    small[base + BIASES : base + BIASES + 8, 0:hidden_width] = total[f_bias : f_bias + 8]
+    chunk = small_own.shape[0]
+    part_of = lambda d: pl.ds(pl.multiple_of(d * chunk, 8), chunk)
+    spread = [
+        sems.copy(small.at[part_of(place.d_at(i)), :], small_in.at[i - 1], {"dp": place.d_at(i)}) for i in range(1, dp)
+    ]
+    for copy in spread:
+        copy.start()
+
+    for copy in row_trades:
+        copy.wait_recv()
+    total = sums[...]
+    for i in range(tensor - 1):
+        total = total + sums_in[i]
+    wide[...] = jnp.zeros_like(wide)
+    wide[0:8, 0:model] = total
+    wide[8:9, 0 : up_sums.shape[1]] = up_sums[...]
+    wide_trades = [sems.copy(wide, wide_in.at[i - 1], {"dp": place.d_at(i)}) for i in range(1, dp)]
+    for copy in wide_trades:
+        copy.start()
+    order = order_matrix(count)
+    grad_tokens[...] = dot(order, near_out[0]).astype(BF16)
+    for copy in spread:
+        copy.wait_recv()
+    total = small[part_of(place.d), :]
+    for i in range(dp - 1):
+        total = total + small_in[i]
+    small_own[...] = total
+    small_all[part_of(place.d), :] = total
+    joined = [sems.copy(small_own, small_all.at[part_of(place.d), :], {"dp": place.d_at(i)}) for i in range(1, dp)]
+    for copy in joined:
+        copy.start()
+    for copy in mlp:
+        copy.wait_recv()
+    copies.take(mlp_loaded)
+    total = mlp_sum[...]
+    for i in range(place.ys - 1):
+        total = total + mlp_in[i].astype(F32)
+    output[...] = dot(order, total.astype(BF16)).astype(BF16)
+    o_down[...] = downs.total()
+    o_up[...] = ups.total()
+    o_out[...] = outs.total()
+    for p in (2, 1, 0):
+        o_in[p] = ins[p].total()
+    for copy in wide_trades:
+        copy.wait_recv()
+    total = wide[...]
+    for i in range(dp - 1):
+        total = total + wide_in[i]
+    o_rows[...] = total
+    for copy in joined:
+        copy.wait_recv()
+    o_small[...] = small_all[0 : base + FIRST, :]
+    o_first[...] = small_all[base + FIRST : base + BIASES + 8, 0:hidden_width]
+    for group in (trades, row_trades, spread, wide_trades, joined, mlp):
+        for copy in group:
+            copy.wait_send()
+    for group in (*gathers, downs, ups, outs, *ins):
+        group.finish()
+    copies.finish()
+
+
+def rear_call(dp, tensor, args, half):
+    S = jax.ShapeDtypeStruct
+    count, model = args[0].shape
+    hidden_width, channels = args[12].shape[1], args[12].shape[2]
+    units = args[3].shape[1]
+    own, cores, rows_d = count // 2, 2 if tensor % 2 == 0 else 1, 4 if dp % 4 == 0 else 1
+    cols_d, ys, rows = dp // rows_d, tensor // cores, model // dp
+    farther = max(ys - 1, 1)
+    base = 2 * hidden_width
+    chunk = -(-(base + BIASES + 8) // (8 * dp)) * 8
+    widest = max(model, units)
+    shapes = mix_shapes(half, channels, hidden_width, 2)
+    V = pltpu.VMEM
+    rows_f = ((count, model), F32)
+    norm = ((2, tensor, own, model), BF16)
+    far = ((farther, count, model), BF16)
+
+    def buffers(lead, last, low):
+        first = [V((*lead, cols_d, rows_d, rows, last), BF16)] if low else []
+        return first + [
+            V((*lead, max(cols_d - 1, 1), rows_d, rows, last), BF16), V((*lead, rows, last), F32),
+            V((*lead, max(rows_d - 1, 1), rows, last), BF16), V((*lead, max(rows_d - 1, 1), rows, last), BF16),
+        ]
+
+    per_t, _ = gather_counts(dp, tensor)
+    copies = 2 * per_t + 6 * (rows_d + cols_d) + 4 * ys + 2 * tensor + 3 * dp
+    hbm = pl.BlockSpec(memory_space=pl.ANY)
+    n_vmem, n_hbm_first = 15, 12
+    specs = vmem_specs(n_vmem) + [hbm] * n_hbm_first + vmem_specs(4) + [hbm] * 7
+    wave, wave_back = args[25], args[26]
     return pl.pallas_call(
-        mixer_backward,
-        out_shape=outs,
-        in_specs=vmem_specs(len(args)),
-        out_specs=vmem_specs(len(outs)),
-        scratch_shapes=[
-            pltpu.VMEM((3, 2, half, width), F32),
-            pltpu.VMEM((3 * half, width), BF16),
-            pltpu.VMEM((6 * half, width), BF16),
-            pltpu.VMEM((6 * half, width), BF16),
-            pltpu.VMEM((2, half, width), F32),
-            pltpu.VMEM((2, 2 * half, width), F32),
-            pltpu.VMEM((2, half // 4, width), F32),
-            pltpu.VMEM((3, 2, half + PAD, width), F32),
-            pltpu.VMEM((2, 2, half, width), F32),
-            pltpu.VMEM((40, width), F32),
+        functools.partial(rear, dp, tensor),
+        out_shape=[
+            S((count, model), BF16), S((count, model), BF16), S((rows, units), F32), S((rows, units), F32),
+            S((3, rows, channels), F32), S((rows, channels), F32), S((base + FIRST, channels), F32),
+            S((BIASES + 8 - FIRST, hidden_width), F32), S((16, widest), F32),
         ],
-        compiler_params=pltpu.CompilerParams(vmem_limit_bytes=VMEM_LIMIT),
-        name="mixer_backward",
+        in_specs=specs,
+        out_specs=vmem_specs(9),
+        scratch_shapes=[V(wave.shape, BF16), V(wave_back.shape, BF16), V((2, half + PAD, 8), F32)]
+        + [V(*v) for v in shapes.values()]
+        + [
+            V(*rows_f), V(*norm), V((2, tensor, own, channels), BF16), V((3, model, channels), BF16), V((model, channels), BF16),
+            V(*norm), V(*far), V((rows_d, rows, units), BF16), V((rows_d, rows, units), BF16),
+            V((3, 2, half, channels), F32), V((6 * half, channels), BF16), V((6 * half, channels), BF16),
+            V((2, half, channels), F32), V((2, 2 * half, channels), F32),
+            V((2, half // 4, channels), F32), V((3, 2, half + PAD, channels), F32),
+            V((3, 2, half, channels), BF16), V((40, channels), F32), V(*rows_f), V((count, 128), F32),
+        ]
+        + buffers((), units, False) + buffers((), units, False) + buffers((3,), channels, True) + buffers((), channels, True)
+        + [V((ys, count, model), F32), V((ys, count, model), BF16), V((ys, count, model), BF16), V(*far), V(*far)]
+        + [
+            V((dp * chunk, channels), F32), V((dp - 1, chunk, channels), F32), V((chunk, channels), F32),
+            V((dp * chunk, channels), F32), V((48 + hidden_width, hidden_width), F32),
+            V((tensor - 1, 48 + hidden_width, hidden_width), F32), V((8, model), F32), V((tensor - 1, 8, model), F32),
+            V((16, widest), F32), V((dp - 1, 16, widest), F32),
+            pltpu.SemaphoreType.DMA((copies,)), pltpu.SemaphoreType.DMA((copies,)), pltpu.SemaphoreType.DMA((20,)),
+        ],
+        compiler_params=pltpu.CompilerParams(collective_id=2, has_side_effects=True, vmem_limit_bytes=63 * 2**20),
+        name="rear",
     )(*args)
-
-
-def smooth_gelu(values):
-    return jax.nn.gelu(values, approximate=True)
 
 
 def body(
@@ -778,159 +1326,59 @@
     down_bias,
     cotangent,
 ):
-    residual = tokens[0].astype(jnp.float32)
-    doc_ids = segment_ids[0]
-    model_width = residual.shape[1]
-    length = doc_ids.shape[0]
     dp, tensor = lax.axis_size("dp"), lax.axis_size("tensor")
-    rows, channels, units, count = in_weight.shape[0], in_weight.shape[2], up_weight.shape[1], tokens.shape[1]
-    half, hidden_width = length // 2, filt_mid_bias.shape[0]
-
-    def take_rows(weight_flat, incoming):
-        product = jnp.dot(incoming, weight_flat, preferred_element_type=jnp.float32)
-        return (product, incoming)
-
-    def back_rows(weight_all, kept_low, incoming):
-        product = jnp.dot(incoming, weight_all, preferred_element_type=jnp.float32)
-        weight_grad = lax.dot_general(
-            incoming, kept_low, COLUMN_CONTRACT, preferred_element_type=jnp.float32
-        )
-        return (product, weight_grad)
-
-    def sum_terms(left_low, weight_all):
-        return lax.dot_general(
-            left_low, weight_all, ROW_CONTRACT, preferred_element_type=jnp.float32
-        )
-
-    normed, first_norm_back = jax.vjp(layer_norm, residual, mix_norm_gain, mix_norm_bias)
-    normed_low = normed.astype(jnp.bfloat16)
-    tables = tuple(jnp.asarray(t) for t in wave_tables(length))
-    ptable = jnp.asarray(position_table(length, filt_in_weight.shape[0]))
+    rows, channels, units = in_weight.shape[0], in_weight.shape[2], up_weight.shape[1]
+    count, model = tokens.shape[1:]
+    length, emb, hidden_width = segment_ids.shape[1], filt_in_weight.shape[0], filt_mid_bias.shape[0]
+    half = length // 2
+    wave, wave_back, *fixed = (jnp.asarray(t) for t in wave_tables(length))
     net = (
-        short_weight, short_bias, ptable, filt_in_weight, filt_in_bias[None], filt_mid_weight,
-        filt_mid_bias[None], jnp.swapaxes(filt_out_weight, 0, 1), decay_rates, long_bias,
+        short_weight, short_bias, jnp.asarray(position_table(length, emb)), filt_in_weight, filt_in_bias[None],
+        filt_mid_weight, filt_mid_bias[None], jnp.swapaxes(filt_out_weight, 0, 1), decay_rates, long_bias,
     )
-    in_par, out_par, up_par, down_par, cot_par, norm_par, gated_par, own_gated, masks, *kept = front_call(
+    w_in, out_par, up_par, down_par, cot_par, norm_par, gated_par, own_gated, masks, *kept = front_call(
         dp, tensor,
-        (tokens[0], cotangent[0], segment_ids, mix_norm_gain[None], mix_norm_bias[None], jnp.swapaxes(in_weight, 0, 1), out_weight,
-         up_weight, down_weight, in_bias) + net + tables,
-        count, model_width, channels, units, rows, half, hidden_width,
+        (tokens[0], cotangent[0], segment_ids, mix_norm_gain[None], mix_norm_bias[None], jnp.swapaxes(in_weight, 0, 1),
+         out_weight, up_weight, down_weight, in_bias) + net + (wave, wave_back, *fixed),
+        count, model, channels, units, rows, half, hidden_width,
     )
-    in_flat = jnp.swapaxes(in_par, 1, 2).reshape(model_width, 3 * channels)
-    out_full = jnp.moveaxis(out_par.reshape(tensor, model_width, channels), 0, 1).reshape(model_width, model_width)
-    out_all = lax.dynamic_index_in_dim(out_par, lax.axis_index("tensor"), 0, False).reshape(model_width, channels)
-    up_all, down_all = up_par.reshape(model_width, units), down_par.reshape(model_width, units)
-    normed_full = in_order(norm_par.reshape(2, half, model_width))
-    cot_full = in_order(cot_par.reshape(2, half, model_width))
-    gated_low = in_order(gated_par.reshape(2, half, channels))
-    own_gated = in_order(jnp.moveaxis(own_gated, 0, 2).reshape(2, count // 2, model_width))
-    mixed = lax.dot_general(own_gated, out_full, ROW_CONTRACT, preferred_element_type=jnp.float32)
-    mixed_sum = residual + mixed + out_bias
-    normed_two, second_norm_back = jax.vjp(layer_norm, mixed_sum, mlp_norm_gain, mlp_norm_bias)
-    normed_two_low = normed_two.astype(jnp.bfloat16)
-    up_raw, normed_two_full = take_rows(
-        up_all, lax.all_gather(normed_two_low, "tensor", axis=0, tiled=True)
+    out_full = out_par.reshape(tensor, model, channels)
+    d_mixed, d_mix_low, mlp_own, mlp_far, g_down, g_up, row_sums, up_sums = middle_call(
+        dp, tensor,
+        (tokens[0], cotangent[0], own_gated, out_full, out_bias[None], mlp_norm_gain[None], mlp_norm_bias[None],
+         up_par.reshape(model, units), up_bias[None], down_par.reshape(model, units), cot_par, down_bias[None]),
     )
-    pre_act = up_raw + up_bias
-    activated, gelu_back = jax.vjp(smooth_gelu, pre_act)
-    act_low = activated.astype(jnp.bfloat16)
-    mlp_sum = lax.psum_scatter(
-        sum_terms(act_low, down_all), "tensor", scatter_dimension=0, tiled=True
+    output, grad_tokens, g_down, g_up, g_in, g_out, small, first, wide = rear_call(
+        dp, tensor,
+        (tokens[0], d_mix_low, row_sums, up_sums, mix_norm_gain[None]) + net
+        + (d_mixed, mlp_own, mlp_far, g_down, g_up, norm_par, gated_par, w_in, out_full, masks, wave, wave_back, *fixed, *kept),
+        half,
     )
-    output = (mixed_sum + mlp_sum + down_bias).astype(jnp.bfloat16)
-    grad_low = cotangent[0]
-    grad_out = grad_low.astype(jnp.float32)
-    grad_down_bias = jnp.sum(grad_out, axis=0)
-    d_act, grad_down = back_rows(
-        down_all, act_low, cot_full
-    )
-    d_pre_low = gelu_back(d_act)[0].astype(jnp.bfloat16)
-    grad_up_bias = jnp.sum(d_pre_low, axis=0, dtype=jnp.float32)
-    grad_up = lax.dot_general(
-        normed_two_full, d_pre_low, COLUMN_CONTRACT, preferred_element_type=jnp.float32
-    )
-    d_normed_two = lax.psum_scatter(
-        sum_terms(d_pre_low, up_all), "tensor", scatter_dimension=0, tiled=True
-    )
-    d_mixed_norm, grad_mlp_gain, grad_mlp_shift = second_norm_back(d_normed_two)
-    d_mixed = grad_out + d_mixed_norm
-    grad_out_bias = jnp.sum(d_mixed, axis=0)
-    d_mix_low = d_mixed.astype(jnp.bfloat16)
-    d_mix_full = lax.all_gather(d_mix_low, "tensor", axis=0, tiled=True)
-    grad_out_w = lax.dot_general(d_mix_full, gated_low, COLUMN_CONTRACT, preferred_element_type=jnp.float32)
-    (
-        d_z_par, grad_in_bias, grad_taps, grad_tap_bias, grad_direct, grad_first_w, grad_first_b, grad_middle_w, grad_middle_b,
-        grad_last_w,
-    ) = backward_call((by_parity(d_mix_full), out_all) + net + (masks,) + tables + tuple(kept), half, channels, filt_in_weight.shape[0], hidden_width)
-    grad_first_b, grad_middle_b = grad_first_b[0], grad_middle_b[0]
-    grad_last_w = jnp.swapaxes(grad_last_w, 0, 1)
-    d_z_low = in_order(jnp.moveaxis(d_z_par, 0, 2)).reshape(length, 3 * channels)
-    grad_in = lax.dot_general(
-        normed_full, d_z_low, COLUMN_CONTRACT, preferred_element_type=jnp.float32
-    ).reshape(model_width, 3, channels)
-    d_normed = lax.psum_scatter(
-        sum_terms(d_z_low, in_flat), "tensor", scatter_dimension=0, tiled=True
-    )
-    d_input_norm, grad_mix_gain, grad_mix_shift = first_norm_back(d_normed)
-    grad_tokens = (d_mixed + d_input_norm).astype(jnp.bfloat16)[None]
-    grad_in, grad_out_w, grad_up, grad_down = (
-        lax.psum_scatter(grad_in, "dp", scatter_dimension=0, tiled=True),
-        lax.psum_scatter(grad_out_w, "dp", scatter_dimension=0, tiled=True),
-        lax.psum_scatter(grad_up, "dp", scatter_dimension=0, tiled=True),
-        lax.psum_scatter(grad_down, "dp", scatter_dimension=0, tiled=True),
-    )
-    grad_in_bias, grad_taps, grad_tap_bias, grad_last_w, grad_direct, grad_up_bias = lax.psum(
-        (grad_in_bias, grad_taps, grad_tap_bias, grad_last_w, grad_direct, grad_up_bias), "dp"
-    )
-    (
-        grad_mix_gain,
-        grad_mix_shift,
-        grad_first_w,
-        grad_first_b,
-        grad_middle_w,
-        grad_middle_b,
-        grad_out_bias,
-        grad_mlp_gain,
-        grad_mlp_shift,
-        grad_down_bias,
-    ) = lax.psum(
-        (
-            grad_mix_gain,
-            grad_mix_shift,
-            grad_first_w,
-            grad_first_b,
-            grad_middle_w,
-            grad_middle_b,
-            grad_out_bias,
-            grad_mlp_gain,
-            grad_mlp_shift,
-            grad_down_bias,
-        ),
-        ("dp", "tensor"),
-    )
+    base = 2 * hidden_width
+    misc = small[base : base + 8]
     return (
         output[None],
-        grad_tokens,
-        grad_mix_gain,
-        grad_mix_shift,
-        grad_in,
-        grad_in_bias,
-        grad_taps,
-        grad_tap_bias,
-        grad_first_w,
-        grad_first_b,
-        grad_middle_w,
-        grad_middle_b,
-        grad_last_w,
-        grad_direct,
-        grad_out_w,
-        grad_out_bias,
-        grad_mlp_gain,
-        grad_mlp_shift,
-        grad_up,
-        grad_up_bias,
-        grad_down,
-        grad_down_bias,
+        grad_tokens[None],
+        wide[0, :model],
+        wide[1, :model],
+        jnp.swapaxes(g_in, 0, 1),
+        misc[0:3],
+        small[base + TAPS : base + TAPS + 9].reshape(3, 3, channels),
+        misc[3:6],
+        first[0:emb],
+        first[BIASES - FIRST],
+        first[SECOND - FIRST : SECOND - FIRST + hidden_width],
+        first[BIASES - FIRST + 1],
+        jnp.swapaxes(small[0:base].reshape(2, hidden_width, channels), 0, 1),
+        misc[6:8],
+        g_out,
+        wide[4, :model],
+        wide[2, :model],
+        wide[3, :model],
+        g_up,
+        wide[8, :units],
+        g_down,
+        wide[5, :model],
     )
 
 

time: 685 us -> 236 us (0.34)
  waiting for transfers between devices: 388 us -> 0 us
  Pallas kernels: 116 us -> 204 us
  blocking collectives: 71.7 us -> 0 us
  matrix products: 35.6 us -> 0 us
  local copies, waits for them, and re-layouts: 42.3 us -> 27.2 us
  between operations: 15 us -> 1.16 us
  other arithmetic: 10.5 us -> 0 us
    reduce_scatter x7 -> x0, waiting for transfers between devices: 348 us -> none  [the longest x1 73 us: body(): lax.psum_scatter(grad_in, 'dp', scatter_dimension=0, tiled=True)]
    pallas_call x1 -> x2, Pallas kernels: 53.3 us -> 142 us  [the longest x1 106 us: rear_call(): pl.pallas_call(functools.partial(rear, dp, tensor), out_shape=[S((count,...]
    psum x2 -> x0, blocking collectives: 71.7 us -> none  [the longest x1 41.2 us: body(): lax.psum((grad_mix_gain, grad_mix_shift, grad_first_w, grad_first_b, grad...]
    all_gather x2 -> x0, waiting for transfers between devices: 39.8 us -> none  [the longest x1 24 us: body(): lax.all_gather(normed_two_low, 'tensor', axis=0, tiled=True)]
    dot_general x10 -> x0, matrix products: 35.6 us -> none  [the longest x3 13.1 us: sum_terms(): lax.dot_general(left_low, weight_all, ROW_CONTRACT, preferred_element_typ...]
    reshape x11 -> x2, local copies, waits for them, and re-layouts: 17.9 us -> 1.37 us  [the longest x1 0.76 us: body(): small[0:base].reshape(2, hidden_width, channels)]
    slice x0 -> x7, local copies, waits for them, and re-layouts: none -> 8.84 us  [the longest x1 1.76 us: body(): wide[5, :model]]
    reduce_sum x7 -> x0, other arithmetic: 8.55 us -> none  [the longest x3 4.57 us: layer_norm(): return centred * lax.rsqrt(spread + EPSILON) * norm_gain + norm_shift]
  transfers between devices with their start and end apart: 10 -> 0, of which waited for: 10 -> 0; matrix products, arithmetic and copies ran while one was open for 8% -> 0% of each run, Pallas kernels for 0% -> 0%
where the time goes in v2:
time: 236 us; the launch traced here: 232 us
  Pallas kernels  204 us (86%)
  local copies, waits for them, and re-layouts  27.2 us (12%)
    pallas_call x1, Pallas kernels, rear_call(): pl.pallas_call(functools.partial(rear, dp, tensor), out_shape=[S((count,...  106 us
    pallas_call x1, Pallas kernels, front_call(): pl.pallas_call(functools.partial(front, dp, tensor), out_shape=outs, in_s...  62.3 us
    pallas_call x1, Pallas kernels, middle_call(): pl.pallas_call(functools.partial(middle, dp, tensor), out_shape=[S(*rows)...  35.7 us
    unnamed x17, local copies, waits for them, and re-layouts  6.88 us

profile of v2, /device:TPU:1, one launch (start us, length us, event | category | flops | bytes accessed | tf_op | source)
XLA Modules:
  0.0 232.4 jit_solution(11476182500882250456)
XLA Ops:
  0.7 1.3 broadcast_in_dim.34.gain
  1.9 1.3 broadcast_in_dim.35.shift
  3.2 1.3 broadcast_in_dim.38.out_bias
  4.5 1.3 broadcast_in_dim.39.gain
  5.7 1.3 broadcast_in_dim.40.shift
  7.0 1.3 broadcast_in_dim.41.up_bias
  8.3 1.3 broadcast_in_dim.42.down_bias
  9.5 1.6 copy.58
  11.1 62.3 %front.1 = (bf16[3,768,192]{2,1,0:T(8,128)(2,1)}, bf16[4,8,96,192]{3,2,1,0:T(8,128)(2,1)}, bf16[8,96,768]{2,1,0:T(8,128)(2,1)}, bf16[8,96,768]{2,1,0:T(8,128)(2,...) custom-call(bf16[256,768]{1,0:T(8,128)(2,1)} %bitcast.24, ...), custom_call_target="tpu_custom_call" | custom-call | tf_op jit(solution)/shard_map/front/pallas_call | solution.py:582
  73.4 35.7 %middle.1 = (f32[256,768]{1,0:T(8,128)}, bf16[256,768]{1,0:T(8,128)(2,1)}, f32[256,768]{1,0:T(8,128)}, bf16[1,256,768]{2,1,0:T(8,128)(2,1)}, bf16[2,4,96,768]{3,...) custom-call(bf16[256,768]{1,0:T(8,128)(2,1)} %bitcast.25, ...), custom_call_target="tpu_custom_call" | custom-call | tf_op jit(solution)/shard_map/middle/pallas_call | solution.py:839
  109.1 106.1 %rear.1 = (bf16[256,768]{1,0:T(8,128)(2,1)}, bf16[256,768]{1,0:T(8,128)(2,1)}, f32[96,768]{1,0:T(8,128)}, f32[96,768]{1,0:T(8,128)}, f32[3,96,192]{2,1,0:T(8,128...) custom-call(bf16[256,768]{1,0:T(8,128)(2,1)} %bitcast.26, ...), custom_call_target="tpu_custom_call" | custom-call | tf_op jit(solution)/shard_map/rear/pallas_call | solution.py:1270
  215.2 0.0 copy-start
  215.2 0.0 copy-start.3
  215.2 0.0 copy-start.4
  215.2 1.3 slice_bitcast_fusion
  216.5 1.3 slice.62
  217.8 1.4 fusion
  219.2 0.7 slice.55
  219.9 0.9 slice.61
  220.8 0.6 reshape.62
  221.4 0.8 copy.57
  222.2 1.4 slice.57
  223.6 1.4 slice.59
  224.9 1.8 slice_reduce_fusion
  226.7 1.8 copy.65
  228.5 0.7 copy.66
  229.2 0.0 copy-done.3
  229.2 0.7 copy.67
  229.9 0.0 copy-done.4
  229.9 0.6 copy.68
  230.6 0.7 copy.69
  231.3 0.7 copy.70
  (5 shorter events, 0.0 us)
Async XLA Ops:
  215.2 13.3 %copy-start = (bf16[256,768]{1,0:T(8,128)(2,1)S(1)}, bf16[256,768]{1,0:T(8,128)(2,1)}, u32[]{:S(2)}) copy-start(bf16[256,768]{1,0:T(8,128)(2,1)} %get-tuple-element.80) | copy-start | bytes 1179652
  215.2 14.0 %copy-start.3 = (f32[3,96,192]{2,1,0:T(8,128)S(1)}, f32[3,96,192]{2,1,0:T(8,128)}, u32[]{:S(2)}) copy-start(f32[3,96,192]{2,1,0:T(8,128)} %get-tuple-element.82) | copy-start | bytes 663556
  215.2 14.7 %copy-start.4 = (f32[96,192]{1,0:T(8,128)S(1)}, f32[96,192]{1,0:T(8,128)}, u32[]{:S(2)}) copy-start(f32[96,192]{1,0:T(8,128)} %get-tuple-element.135) | copy-start | bytes 221188
  216.5 14.1 %copy-start.2 = (f32[96,768]{1,0:T(8,128)S(1)}, f32[96,768]{1,0:T(8,128)}, u32[]{:S(2)}) copy-start(f32[96,768]{1,0:T(8,128)} %get-tuple-element.139) | copy-start | bytes 884740
  222.2 9.1 %copy-start.1 = (f32[96,768]{1,0:T(8,128)S(1)}, f32[96,768]{1,0:T(8,128)}, u32[]{:S(2)}) copy-start(f32[96,768]{1,0:T(8,128)} %get-tuple-element.141) | copy-start | bytes 884740
